TPU v7x, 32 devices: a whole 2x2x4 slice. The times are simulated.
32 devices in a mesh: narrow: 4 (over y, x), wide: 8 (over z, core).
Axes of the slice: x: 2, y: 2, z: 4, core: 2. Of those that a mesh axis runs over, the one named last changes fastest.
Arguments:
- hidden_in: bfloat16 [16, 2048, 768], P('wide', 'narrow'), may hold values from -6 to 6
- lengths: int32 [16], P('wide'), may hold values from 512 to 2048, as said below
- routes: int32 [16, 2048, 1], P('wide', 'narrow'), may hold values from 0 to 15
- norm_gain_attn: float32 [768], replicated, may hold values from 0.5 to 1.5
- query_weight: bfloat16 [768, 768], replicated, may hold values from -0.21875 to 0.21875
- key_weight: bfloat16 [768, 768], replicated, may hold values from -0.21875 to 0.21875
- value_weight: bfloat16 [768, 768], replicated, may hold values from -0.21875 to 0.21875
- out_weight: bfloat16 [768, 768], replicated, may hold values from -0.875 to 0.875
- bias_table: float32 [32, 12], replicated, may hold values from -4 to 4
- norm_gain_ffn: float32 [768], replicated, may hold values from 0.5 to 1.5
- router_weight: bfloat16 [768, 16], replicated, may hold values from -0.109375 to 0.109375
- expert_in: bfloat16 [16, 768, 3072], P('wide', None, 'narrow'), may hold values from -0.21875 to 0.21875
- expert_out: bfloat16 [16, 3072, 768], P('wide', 'narrow'), may hold values from -6 to 6
- cotangent: bfloat16 [16, 2048, 768], P('wide', 'narrow'), may hold values from -6 to 6
Outputs:
- block_out: float32 [16, 2048, 768], P('wide', 'narrow')
- grad_hidden: float32 [16, 2048, 768], P('wide', 'narrow')
- grad_gain_attn: float32 [768], replicated
- grad_query: float32 [768, 768], replicated
- grad_key: float32 [768, 768], replicated
- grad_value: float32 [768, 768], replicated
- grad_out: float32 [768, 768], replicated
- grad_table: float32 [32, 12], replicated
- grad_gain_ffn: float32 [768], replicated
- grad_router: float32 [768, 16], replicated
- grad_expert_in: float32 [16, 768, 3072], P('wide', None, 'narrow')
- grad_expert_out: float32 [16, 3072, 768], P('wide', 'narrow')
Inputs may be any that keep to these rules, and one draw needn't show every extreme that they name: `lengths`: each length lies between 512 and 2048; in every aligned block of 2 sequences one has exactly 2048.
All inputs are finite; a program needn't handle non-finite values.
Results may differ from a plain program's by a relative error of at most 0.015.
Values may be sent and summed in bfloat16 or wider, within the bound.
No kernel may reach another device: no remote copies, remote signals or barrier semaphores. Data moves between devices by JAX's collectives and lax.ppermute only.
A program may use at most 448 MiB of HBM per device.

v0:
```python
import jax
import jax.numpy as jnp
from jax import lax
from jax.sharding import PartitionSpec as P

epsilon = 1e-06
masked_score = -1000000000.0
bucket_edges = (1, 2, 3, 4, 5, 6, 7, 8, 12, 16, 23, 32, 46, 64, 91)


def rms_norm(values, gain_vector):
    factor = lax.rsqrt(jnp.mean(values * values, axis=-1, keepdims=True) + epsilon)
    return values * factor * gain_vector


def bucket_of(offsets):
    magnitude = jnp.abs(offsets)
    bucket = jnp.zeros_like(offsets)
    for border in bucket_edges:
        bucket = bucket + (magnitude >= border).astype(jnp.int32)
    return bucket


def gelu_exact(values):
    return jax.nn.gelu(values, approximate=False)


def on_device(
    hidden_in,
    lengths,
    routes,
    norm_gain_attn,
    query_weight,
    key_weight,
    value_weight,
    out_weight,
    bias_table,
    norm_gain_ffn,
    router_weight,
    expert_in,
    expert_out,
    cotangent,
):
    narrow_count = lax.axis_size("narrow")
    wide_count = lax.axis_size("wide")
    seq_count, own_rows, model_width = hidden_in.shape
    bucket_count, head_count = bias_table.shape
    head_size = model_width // head_count
    full_length = own_rows * narrow_count
    token_count = seq_count * own_rows
    local_experts = expert_in.shape[0]
    expert_count = local_experts * wide_count
    capacity = 5 * token_count // (4 * expert_count)
    slot_count = expert_count * capacity
    first_row = lax.axis_index("narrow") * own_rows
    source = hidden_in.astype(jnp.float32).reshape(token_count, model_width)
    normed_attn = rms_norm(source, norm_gain_attn).astype(jnp.bfloat16)
    joined_weight = jnp.concatenate((query_weight, key_weight, value_weight), axis=1)
    projected = jnp.dot(normed_attn, joined_weight, preferred_element_type=jnp.float32).astype(
        jnp.bfloat16
    )
    queries = projected[:, :model_width].reshape(seq_count, own_rows, model_width)
    own_pairs = projected[:, model_width:].reshape(seq_count, own_rows, 2 * model_width)
    all_pairs = lax.all_gather(own_pairs, "narrow", axis=1, tiled=True)
    query_pos = first_row + jnp.arange(own_rows, dtype=jnp.int32)
    key_pos = jnp.arange(full_length, dtype=jnp.int32)
    offsets = key_pos[None, :] - query_pos[:, None]
    bucket_grid = bucket_of(offsets) + bucket_count // 2 * (offsets > 0).astype(jnp.int32)
    bias_block = jnp.zeros((head_count, own_rows, full_length), jnp.float32)
    for bucket_id in range(bucket_count):
        bias_block = jnp.where(
            (bucket_grid == bucket_id)[None, :, :], bias_table[bucket_id][:, None, None], bias_block
        )
    bucket_onehot = (
        jnp.arange(bucket_count, dtype=jnp.int32)[:, None]
        == bucket_grid.reshape(1, own_rows * full_length)
    ).astype(jnp.bfloat16)

    def score_block(query_seq, pair_seq, length_one):
        query_heads = query_seq.reshape(own_rows, head_count, head_size)
        key_heads = pair_seq[:, :model_width].reshape(full_length, head_count, head_size)
        value_heads = pair_seq[:, model_width:].reshape(full_length, head_count, head_size)
        scores = (
            jnp.einsum("qhd,khd->hqk", query_heads, key_heads, preferred_element_type=jnp.float32)
            * 0.125
        )
        scores = scores + bias_block
        usable = (key_pos < length_one)[None, None, :]
        return (
            query_heads,
            key_heads,
            value_heads,
            jnp.where(usable, scores, masked_score),
            usable,
        )

    def attend_forward(inputs):
        query_seq, pair_seq, length_one = inputs
        pieces = score_block(query_seq, pair_seq, length_one)
        value_heads, scores, usable = (pieces[2], pieces[3], pieces[4])
        row_max = jnp.max(scores, axis=-1, keepdims=True)
        weights = jnp.where(usable, jnp.exp(scores - row_max), 0.0)
        totals = jnp.sum(weights, axis=-1, keepdims=True)
        attn_probs = (weights / totals).astype(jnp.bfloat16)
        attended_seq = jnp.einsum(
            "hqk,khd->qhd", attn_probs, value_heads, preferred_element_type=jnp.float32
        )
        log_total = row_max[..., 0] + jnp.log(totals[..., 0])
        return (attended_seq.astype(jnp.bfloat16).reshape(own_rows, model_width), log_total)

    attended, log_totals = lax.map(attend_forward, (queries, all_pairs, lengths))
    attended_flat = attended.reshape(token_count, model_width)
    branch = jnp.dot(attended_flat, out_weight, preferred_element_type=jnp.float32)
    residual = source + branch
    ffn_input = rms_norm(residual, norm_gain_ffn).astype(jnp.bfloat16)
    logits = jnp.dot(ffn_input, router_weight, preferred_element_type=jnp.float32)
    router_probs = jax.nn.softmax(logits, axis=-1)
    route_flat = routes.reshape(token_count)
    live_mask = (query_pos[None, :] < lengths[:, None]).reshape(token_count).astype(jnp.float32)
    expert_ids = jnp.arange(expert_count, dtype=jnp.int32)
    chosen = (route_flat[:, None] == expert_ids[None, :]).astype(jnp.float32) * live_mask[:, None]
    gate_value = jnp.sum(router_probs * chosen, axis=-1)
    token_ids = jnp.arange(token_count, dtype=jnp.int32)
    earlier = (token_ids[:, None] > token_ids[None, :]).astype(jnp.bfloat16)
    before = jnp.dot(earlier, chosen.astype(jnp.bfloat16), preferred_element_type=jnp.float32)
    place_index = jnp.sum(before * chosen, axis=-1).astype(jnp.int32)
    kept_mask = (live_mask > 0.5) & (place_index < capacity)
    slot_index = route_flat * capacity + place_index
    slot_ids = jnp.arange(slot_count, dtype=jnp.int32)
    dispatch_map = ((slot_ids[:, None] == slot_index[None, :]) & kept_mask[None, :]).astype(
        jnp.bfloat16
    )
    send_rows = jnp.dot(dispatch_map, ffn_input, preferred_element_type=jnp.float32).astype(
        jnp.bfloat16
    )
    send_rows = send_rows.reshape(wide_count, local_experts, capacity, model_width)
    whole_in, whole_out = (
        lax.all_gather(expert_in, "narrow", axis=2, tiled=True),
        lax.all_gather(expert_out, "narrow", axis=1, tiled=True),
    )
    slot_rows = lax.all_to_all(send_rows, "wide", split_axis=0, concat_axis=0, tiled=True)
    pre_act = jnp.einsum("wekd,edf->wekf", slot_rows, whole_in, preferred_element_type=jnp.float32)
    hidden = gelu_exact(pre_act).astype(jnp.bfloat16)
    output = jnp.einsum("wekf,efd->wekd", hidden, whole_out, preferred_element_type=jnp.float32)
    returned_rows = lax.all_to_all(
        output.astype(jnp.bfloat16), "wide", split_axis=0, concat_axis=0, tiled=True
    )
    token_result = jnp.einsum(
        "st,sd->td",
        dispatch_map,
        returned_rows.reshape(slot_count, model_width),
        preferred_element_type=jnp.float32,
    )
    block_out = residual + gate_value[:, None] * token_result
    grad_top = cotangent.astype(jnp.float32).reshape(token_count, model_width)
    grad_tokens = (gate_value[:, None] * grad_top).astype(jnp.bfloat16)
    grad_slots = jnp.dot(dispatch_map, grad_tokens, preferred_element_type=jnp.float32).astype(
        jnp.bfloat16
    )
    grad_recv = lax.all_to_all(
        grad_slots.reshape(wide_count, local_experts, capacity, model_width),
        "wide",
        split_axis=0,
        concat_axis=0,
        tiled=True,
    )
    pre_act = jnp.einsum("wekd,edf->wekf", slot_rows, whole_in, preferred_element_type=jnp.float32)
    hidden, gelu_pull = jax.vjp(gelu_exact, pre_act)
    hidden_low = hidden.astype(jnp.bfloat16)
    grad_units = jnp.einsum(
        "wekd,efd->wekf", grad_recv, whole_out, preferred_element_type=jnp.float32
    )
    grad_pre = gelu_pull(grad_units)[0].astype(jnp.bfloat16)
    grad_rows_part = jnp.einsum(
        "wekf,edf->wekd", grad_pre, whole_in, preferred_element_type=jnp.float32
    )
    grad_expert_in = jnp.einsum(
        "wekd,wekf->edf", slot_rows, grad_pre, preferred_element_type=jnp.float32
    )
    grad_expert_out = jnp.einsum(
        "wekf,wekd->efd", hidden_low, grad_recv, preferred_element_type=jnp.float32
    )
    grad_expert_in, grad_expert_out = (
        lax.psum_scatter(
            grad_expert_in.astype(jnp.bfloat16), "narrow", scatter_dimension=2, tiled=True
        ).astype(jnp.float32),
        lax.psum_scatter(
            grad_expert_out.astype(jnp.bfloat16), "narrow", scatter_dimension=1, tiled=True
        ).astype(jnp.float32),
    )
    grad_back = lax.all_to_all(
        grad_rows_part.astype(jnp.bfloat16), "wide", split_axis=0, concat_axis=0, tiled=True
    )
    grad_from_experts = jnp.einsum(
        "st,sd->td",
        dispatch_map,
        grad_back.reshape(slot_count, model_width),
        preferred_element_type=jnp.float32,
    )
    grad_gate = jnp.sum(grad_top * token_result, axis=-1)
    grad_probs = chosen * grad_gate[:, None]
    grad_logits = router_probs * (
        grad_probs - jnp.sum(router_probs * grad_probs, axis=-1, keepdims=True)
    )
    grad_logits = grad_logits.astype(jnp.bfloat16)
    grad_ffn_input = grad_from_experts + jnp.einsum(
        "te,de->td", grad_logits, router_weight, preferred_element_type=jnp.float32
    )
    grad_router = jnp.einsum(
        "td,te->de", ffn_input, grad_logits, preferred_element_type=jnp.float32
    )
    ffn_pull = jax.vjp(rms_norm, residual, norm_gain_ffn)[1]
    grad_residual_norm, grad_gain_ffn = ffn_pull(grad_ffn_input)
    grad_residual = grad_top + grad_residual_norm
    grad_branch = grad_residual.astype(jnp.bfloat16)
    grad_out_weight = jnp.einsum(
        "td,te->de", attended_flat, grad_branch, preferred_element_type=jnp.float32
    )
    grad_attended = jnp.einsum(
        "te,de->td", grad_branch, out_weight, preferred_element_type=jnp.float32
    )
    grad_attended = grad_attended.astype(jnp.bfloat16).reshape(seq_count, own_rows, model_width)

    def attend_backward(table_sum, inputs):
        query_seq, pair_seq, length_one, log_total, grad_seq = inputs
        query_heads, key_heads, value_heads, scores, usable = score_block(
            query_seq, pair_seq, length_one
        )
        attn_probs = jnp.where(usable, jnp.exp(scores - log_total[..., None]), 0.0)
        grad_heads = grad_seq.reshape(own_rows, head_count, head_size)
        grad_dot = jnp.einsum(
            "qhd,khd->hqk", grad_heads, value_heads, preferred_element_type=jnp.float32
        )
        grad_scores = attn_probs * (
            grad_dot - jnp.sum(attn_probs * grad_dot, axis=-1, keepdims=True)
        )
        grad_scores = grad_scores.astype(jnp.bfloat16)
        grad_query = (
            jnp.einsum("hqk,khd->qhd", grad_scores, key_heads, preferred_element_type=jnp.float32)
            * 0.125
        )
        grad_key = (
            jnp.einsum("hqk,qhd->khd", grad_scores, query_heads, preferred_element_type=jnp.float32)
            * 0.125
        )
        grad_value = jnp.einsum(
            "hqk,qhd->khd",
            attn_probs.astype(jnp.bfloat16),
            grad_heads,
            preferred_element_type=jnp.float32,
        )
        grad_pair = jnp.concatenate(
            (
                grad_key.reshape(full_length, model_width),
                grad_value.reshape(full_length, model_width),
            ),
            axis=1,
        )
        query_part = grad_query.astype(jnp.bfloat16).reshape(own_rows, model_width)
        table_part = jnp.einsum(
            "bn,hn->bh",
            bucket_onehot,
            grad_scores.reshape(head_count, own_rows * full_length),
            preferred_element_type=jnp.float32,
        )
        return (table_sum + table_part, (query_part, grad_pair))

    grad_table, (grad_queries, grad_pairs) = lax.scan(
        attend_backward,
        jnp.zeros((bucket_count, head_count), jnp.float32),
        (queries, all_pairs, lengths, log_totals, grad_attended),
    )
    own_grad_pairs = lax.psum_scatter(
        grad_pairs.astype(jnp.bfloat16), "narrow", scatter_dimension=1, tiled=True
    )
    grad_joined = jnp.concatenate(
        (
            grad_queries.reshape(token_count, model_width),
            own_grad_pairs.reshape(token_count, 2 * model_width),
        ),
        axis=1,
    )
    grad_joined_weight = jnp.einsum(
        "td,te->de", normed_attn, grad_joined, preferred_element_type=jnp.float32
    )
    grad_normed = jnp.einsum(
        "te,de->td", grad_joined, joined_weight, preferred_element_type=jnp.float32
    )
    source_pull = jax.vjp(rms_norm, source, norm_gain_attn)[1]
    grad_source, grad_gain_attn = source_pull(grad_normed)
    grad_hidden = grad_residual + grad_source
    summed = lax.psum(
        (
            grad_joined_weight,
            grad_out_weight,
            grad_router,
            grad_table,
            grad_gain_attn,
            grad_gain_ffn,
        ),
        ("narrow", "wide"),
    )
    joined_sum = summed[0]
    out_shape = (seq_count, own_rows, model_width)
    return (
        block_out.reshape(out_shape),
        grad_hidden.reshape(out_shape),
        summed[4],
        joined_sum[:, :model_width],
        joined_sum[:, model_width : 2 * model_width],
        joined_sum[:, 2 * model_width :],
        summed[1],
        summed[3],
        summed[5],
        summed[2],
        grad_expert_in,
        grad_expert_out,
    )


def solution(mesh):
    placed = (
        P("wide", "narrow", None),
        P("wide"),
        P("wide", "narrow", None),
        P(),
        P(),
        P(),
        P(),
        P(),
        P(),
        P(),
        P(),
        P("wide", None, "narrow"),
        P("wide", "narrow", None),
        P("wide", "narrow", None),
    )
    return jax.shard_map(
        on_device,
        mesh=mesh,
        in_specs=placed,
        out_specs=(
            P("wide", "narrow", None),
            P("wide", "narrow", None),
            P(),
            P(),
            P(),
            P(),
            P(),
            P(),
            P(),
            P(),
            P("wide", None, "narrow"),
            P("wide", "narrow", None),
        ),
        check_vma=False,
    )
```

profile of v0, /device:TPU:0, one launch (start us, length us, event | category | flops | bytes accessed | tf_op | source)
XLA Modules:
  0.0 2122.9 jit_solution(4668477671842769752)
XLA Ops:
  30.1 36.1 %convert_bitcast_fusion.2 = (s32[64,16,8,128]{3,2,1,0:T(8,128)}, pred[512,2048]{1,0:T(8,128)(4,1)}, pred[512,2048]{1,0:T(8,128)(4,1)}, pred[512,2048]{1,0:T(8,12...) fusion(s32[512]{0:T(512)S(1)} %iota_add_fusion), kind=kLoop, calls=%fused_computation.89 | loop fusion | flops 84934656 | bytes 46139392
  67.8 82.6 %all-gather.4.cloned.1.call-done = bf16[2,2048,1536]{1,2,0:T(8,128)(2,1)} async-done(((bf16[2,512,1536]{1,2,0:T(8,128)(2,1)}), bf16[2,2048,1536]{1,2,0:T(8,128)(2,1)}) %all-gather.4.cloned.1.call-update) | async-done | bytes 12582928 | tf_op jit(solution)/shard_map/all_gather | solution.py:64
  151.6 388.4 %while.28 = (s32[]{:T(128)}, bf16[2,512,768]{2,1,0:T(8,128)(2,1)}, f32[2,12,512]{2,1,0:T(8,128)}, bf16[2,2048,1536]{1,2,0:T(8,128)(2,1)}, s32[2]{0:T(128)}, /*in...) while((s32[]{:T(128)}, bf16[2,512,768]{2,1,0:T(8,128)(2,1)}, ...), condition=%wide.region_4.5_spmd.clone, body=%wide.region_1.4_spmd.clone.sunk | while | flops 3762679808 | bytes 264866192 | solution.py:111
  177.8 134.3 %fusion.219 = (f32[12,512]{1,0:T(8,128)S(1)}, f32[12,512,2048]{2,1,0:T(8,128)}) fusion(f32[12]{0:T(128)S(1)} %get-tuple-element.2482, pred[512,2048]{1,0:T(8,128)(4,1)} %get-tuple-element.2483, f32[12]{0:T(128)S(1)} %get-tuple-element.2484, pred[512,2048]{1,0:T(8,128)(4,1)} %get-tuple-element.2485, f32[12]{0:T(128)S(1)} %get-tuple-element.2486, ...), kind=kOutput, calls=%fused_computation.272.clone.1 | convolution fusion | flops 2063591424 | bytes 87846400 | tf_op jit(solution)/shard_map/while/body/eval_jaxpr/qhd,khd->hqk/dot_general | solution.py:84
  312.0 20.7 fusion.220
  332.8 19.3 fusion.221
  364.0 134.3 %fusion.219 = (f32[12,512]{1,0:T(8,128)S(1)}, f32[12,512,2048]{2,1,0:T(8,128)}) fusion(f32[12]{0:T(128)S(1)} %get-tuple-element.2482, pred[512,2048]{1,0:T(8,128)(4,1)} %get-tuple-element.2483, f32[12]{0:T(128)S(1)} %get-tuple-element.2484, pred[512,2048]{1,0:T(8,128)(4,1)} %get-tuple-element.2485, f32[12]{0:T(128)S(1)} %get-tuple-element.2486, ...), kind=kOutput, calls=%fused_computation.272.clone.1 | convolution fusion | flops 2063591424 | bytes 87846400 | tf_op jit(solution)/shard_map/while/body/eval_jaxpr/qhd,khd->hqk/dot_general | solution.py:84
  498.3 20.7 fusion.220
  519.1 19.3 fusion.221
  554.0 46.3 %all-to-all-done = bf16[8,2,80,768]{3,2,1,0:T(8,128)(2,1)} async-done(((bf16[8,2,80,768]{3,2,1,0:T(8,128)(2,1)}), bf16[8,2,80,768]{3,2,1,0:T(8,128)(2,1)}, u32[]{:S(2)}, u32[]{:S(2)}) %all-to-all-start) | async-done | bytes 1966112 | tf_op jit(solution)/shard_map/all_to_all | solution.py:141
  600.3 42.8 %fusion.40 = (bf16[8,2,80,3072]{3,2,0,1:T(8,128)(2,1)}, f32[8,2,80,3072]{3,2,0,1:T(8,128)}, f32[2,8,80,3072]{3,2,1,0:T(8,128)}) fusion(bf16[2,768,3072]{2,1,0:T(8,128)(2,1)} %all-gather.6.cloned.1.call-done, bf16[8,2,80,768]{3,2,1,0:T(8,128)(2,1)} %all-to-all-done), kind=kOutput, calls=%fused_computation.62 | convolution fusion | flops 6295388160 | bytes 50724864 | tf_op jit(solution)/shard_map/wekd,edf->wekf/dot_general | solution.py:142
  643.1 11.3 convert_bitcast_fusion.4
  661.0 45.6 %all-to-all-done.1 = bf16[8,2,80,768]{3,2,1,0:T(8,128)(2,1)} async-done(((bf16[8,2,80,768]{3,2,1,0:T(8,128)(2,1)}), bf16[8,2,80,768]{3,2,1,0:T(8,128)(2,1)}, u32[]{:S(2)}, u32[]{:S(2)}) %all-to-all-start.1) | async-done | bytes 1966112 | tf_op jit(solution)/shard_map/all_to_all | solution.py:145
  741.4 25.8 %all-to-all-done.2 = bf16[8,2,80,768]{3,2,1,0:T(8,128)(2,1)S(1)} async-done(((bf16[8,2,80,768]{3,2,1,0:T(8,128)(2,1)}), bf16[8,2,80,768]{3,2,1,0:T(8,128)(2,1)S(1)}, u32[]{:S(2)}, u32[]{:S(2)}) %all-to-all-start.2) | async-done | bytes 1966112 | tf_op jit(solution)/shard_map/all_to_all | solution.py:160
  767.2 22.5 %fusion.37 = bf16[8,2,80,3072]{3,2,0,1:T(8,128)(2,1)} fusion(f32[8,2,80,3072]{3,2,0,1:T(8,128)} %get-tuple-element.1392, f32[2,8,80,3072]{3,2,1,0:T(8,128)} %get-tuple-element.1445, bf16[2,3072,768]{2,1,0:T(8,128)(2,1)} %all-gather.8.cloned.1.call-done, bf16[8,2,80,768]{3,2,1,0:T(8,128)(2,1)S(1)} %all-to-all-done.2), kind=kOutput, calls=%fused_computation.54 | convolution fusion | flops 6094848000 | bytes 50724864 | tf_op jit(solution)/shard_map/wekd,efd->wekf/dot_general | solution.py:170
  789.7 11.4 convert_bitcast_fusion.3
  806.2 10.0 add_add_fusion.2
  816.2 36.1 %all-to-all-done.3 = bf16[8,2,80,768]{3,2,1,0:T(8,128)(2,1)S(1)} async-done(((bf16[8,2,80,768]{3,2,1,0:T(8,128)(2,1)}), bf16[8,2,80,768]{3,2,1,0:T(8,128)(2,1)S(1)}, u32[]{:S(2)}, u32[]{:S(2)}) %all-to-all-start.3) | async-done | bytes 1966112 | tf_op jit(solution)/shard_map/all_to_all | solution.py:191
  864.0 730.4 %while.29 = (s32[]{:T(128)}, f32[32,12]{0,1:T(8,128)}, bf16[2,512,768]{2,1,0:T(8,128)(2,1)}, bf16[2,2048,1536]{2,1,0:T(8,128)(2,1)}, s32[2]{0:T(128)}, /*index=5...) while((s32[]{:T(128)}, f32[32,12]{0,1:T(8,128)}, ...), condition=%wide.region_15.16_spmd.clone, body=%wide.region_13.15_spmd.clone.sunk | while | flops 9483056128 | bytes 688278912 | solution.py:268
  875.7 21.2 %fusion.235 = f32[12,512,2048]{2,1,0:T(8,128)} fusion(bf16[512,12,64]{0,2,1:T(8,128)(2,1)S(1)} %bitcast.311, bf16[2048,12,64]{0,2,1:T(8,128)(2,1)} %bitcast.308), kind=kOutput, calls=%fused_computation.276.clone.1 | convolution fusion | flops 1610612736 | bytes 54263808 | tf_op jit(solution)/shard_map/while/body/eval_jaxpr/qhd,khd->hqk/dot_general | solution.py:231
  897.2 145.6 %multiply_reduce_fusion.5 = (f32[12,512]{1,0:T(8,128)S(1)}, f32[12,512,2048]{2,1,0:T(8,128)}) fusion(f32[12,512,2048]{2,1,0:T(8,128)} %fusion.235, f32[12,512]{1,0:T(8,128)S(1)} %dynamic-slice_bitcast_fusion.8, f32[12]{0:T(128)S(1)} %copy-done.99, pred[512,2048]{1,0:T(8,128)(4,1)} %get-tuple-element.2711, f32[12]{0:T(128)S(1)} %copy-done.101, ...), kind=kOutput, calls=%fused_computation.28.clone.1 | convolution fusion | flops 2101340160 | bytes 138202624 | tf_op jit(solution)/shard_map/while/body/eval_jaxpr/qhd,khd->hqk/dot_general | solution.py:84
  1042.8 40.1 %multiply_convert_fusion.5 = bf16[12,512,2048]{2,1,0:T(8,128)(2,1)} fusion(f32[12,512,2048]{2,1,0:T(8,128)} %get-tuple-element.2332, f32[12,512,2048]{2,1,0:T(8,128)} %fusion.235, f32[12,512]{1,0:T(8,128)S(1)} %get-tuple-element.2333), kind=kLoop, calls=%fused_computation.27.clone.1 | loop fusion | flops 37748736 | bytes 125853696 | tf_op jit(solution)/shard_map/while/body/eval_jaxpr/convert_element_type | solution.py:237
  1082.9 18.7 fusion.237
  1101.6 13.4 multiply_convert_fusion.6
  1116.2 12.8 convolution_multiply_fusion.2
  1132.7 8.6 copy.106
  1147.3 20.2 pad.22
  1167.5 30.2 %copy.104 = bf16[2,8,512,2048]{3,1,2,0:T(8,128)(2,1)} copy(bf16[2,8,512,2048]{3,2,1,0:T(8,128)(2,1)} %bitcast.304) | data formatting | bytes 67108864 | tf_op jit(solution)/shard_map/while
  1197.6 21.7 %fusion.236 = f32[32,12]{0,1:T(8,128)S(1)} fusion(bf16[12,1048576]{1,0:T(8,128)(2,1)} %bitcast.305, s32[1048576]{0:T(1024)} %get-tuple-element.2774, f32[32,12]{0,1:T(8,128)S(1)} %copy-done.71, pred[]{:T(512)S(6)} %compare.3), kind=kOutput, calls=%fused_computation.36.clone.1 | convolution fusion | flops 872416000 | bytes 29363200 | tf_op jit(solution)/shard_map/while/body/eval_jaxpr/bn,hn->bh/dot_general | solution.py:260
  1231.7 21.2 %fusion.235 = f32[12,512,2048]{2,1,0:T(8,128)} fusion(bf16[512,12,64]{0,2,1:T(8,128)(2,1)S(1)} %bitcast.311, bf16[2048,12,64]{0,2,1:T(8,128)(2,1)} %bitcast.308), kind=kOutput, calls=%fused_computation.276.clone.1 | convolution fusion | flops 1610612736 | bytes 54263808 | tf_op jit(solution)/shard_map/while/body/eval_jaxpr/qhd,khd->hqk/dot_general | solution.py:231
  1253.2 157.5 %multiply_reduce_fusion.5 = (f32[12,512]{1,0:T(8,128)S(1)}, f32[12,512,2048]{2,1,0:T(8,128)}) fusion(f32[12,512,2048]{2,1,0:T(8,128)} %fusion.235, f32[12,512]{1,0:T(8,128)S(1)} %dynamic-slice_bitcast_fusion.8, f32[12]{0:T(128)S(1)} %copy-done.99, pred[512,2048]{1,0:T(8,128)(4,1)} %get-tuple-element.2711, f32[12]{0:T(128)S(1)} %copy-done.101, ...), kind=kOutput, calls=%fused_computation.28.clone.1 | convolution fusion | flops 2101340160 | bytes 138202624 | tf_op jit(solution)/shard_map/while/body/eval_jaxpr/qhd,khd->hqk/dot_general | solution.py:84
  1410.7 40.1 %multiply_convert_fusion.5 = bf16[12,512,2048]{2,1,0:T(8,128)(2,1)} fusion(f32[12,512,2048]{2,1,0:T(8,128)} %get-tuple-element.2332, f32[12,512,2048]{2,1,0:T(8,128)} %fusion.235, f32[12,512]{1,0:T(8,128)S(1)} %get-tuple-element.2333), kind=kLoop, calls=%fused_computation.27.clone.1 | loop fusion | flops 37748736 | bytes 125853696 | tf_op jit(solution)/shard_map/while/body/eval_jaxpr/convert_element_type | solution.py:237
  1450.8 18.7 fusion.237
  1469.5 13.4 multiply_convert_fusion.6
  1484.1 12.8 convolution_multiply_fusion.2
  1500.7 8.6 copy.106
  1515.1 20.2 pad.22
  1535.3 30.2 %copy.104 = bf16[2,8,512,2048]{3,1,2,0:T(8,128)(2,1)} copy(bf16[2,8,512,2048]{3,2,1,0:T(8,128)(2,1)} %bitcast.304) | data formatting | bytes 67108864 | tf_op jit(solution)/shard_map/while
  1565.5 21.9 %fusion.236 = f32[32,12]{0,1:T(8,128)S(1)} fusion(bf16[12,1048576]{1,0:T(8,128)(2,1)} %bitcast.305, s32[1048576]{0:T(1024)} %get-tuple-element.2774, f32[32,12]{0,1:T(8,128)S(1)} %copy-done.71, pred[]{:T(512)S(6)} %compare.3), kind=kOutput, calls=%fused_computation.36.clone.1 | convolution fusion | flops 872416000 | bytes 29363200 | tf_op jit(solution)/shard_map/while/body/eval_jaxpr/bn,hn->bh/dot_general | solution.py:260
  1594.5 12.7 bitcast_convert_fusion.1
  1608.8 15.5 bitcast_convert_fusion
  1629.7 83.5 %reduce-scatter.4.cloned.1.call-done = bf16[2,512,1536]{2,1,0:T(8,128)(2,1)} async-done(((bf16[2,2048,1536]{2,1,0:T(8,128)(2,1)}), bf16[2,512,1536]{2,1,0:T(8,128)(2,1)}) %reduce-scatter.4.cloned.1.call-update) | async-done | bytes 3145744 | tf_op jit(solution)/shard_map/reduce_scatter | solution.py:273
  1713.3 8.4 fusion.106
  1723.9 87.3 %reduce-scatter.6.cloned.1.call-done = bf16[2,768,768]{2,1,0:T(8,128)(2,1)} async-done(((bf16[2,768,3072]{2,1,0:T(8,128)(2,1)}), bf16[2,768,768]{2,1,0:T(8,128)(2,1)}) %reduce-scatter.6.cloned.1.call-update) | async-done | bytes 2359312 | tf_op jit(solution)/shard_map/reduce_scatter | solution.py:184
  1815.4 93.8 %reduce-scatter.8.cloned.1.call-done = bf16[2,768,768]{2,1,0:T(8,128)(2,1)} async-done(((bf16[2,3072,768]{2,1,0:T(8,128)(2,1)}), bf16[2,768,768]{2,1,0:T(8,128)(2,1)}) %reduce-scatter.8.cloned.1.call-update) | async-done | bytes 2359312 | tf_op jit(solution)/shard_map/reduce_scatter | solution.py:187
  1914.1 7.2 fusion.103
  1921.3 42.5 %all-reduce = (f32[768]{0:T(1024)}, f32[32,12]{0,1:T(8,128)}, f32[768]{0:T(1024)}, f32[768,16]{0,1:T(8,128)}) all-reduce(f32[768]{0:T(1024)S(1)} %get-tuple-element.1061, f32[32,12]{0,1:T(8,128)S(1)} %copy-done.73, f32[768]{0:T(1024)S(1)} %copy-done.68, ...), channel_id=1, replica_groups=mesh['narrow'=4,'wide'=8] {'narrow','wide'}, use_global_device_ids=true, to_apply=%region_19.20 | all-reduce | flops 14208 | bytes 113664 | tf_op jit(solution)/shard_map/psum | solution.py:292
  1969.2 138.9 %all-reduce.4.cloned.1.call-done = (f32[768,2304]{1,0:T(8,128)}, f32[768,768]{1,0:T(8,128)}) async-done(((f32[768,2304]{1,0:T(8,128)}, f32[768,768]{1,0:T(8,128)}), (f32[768,2304]{1,0:T(8,128)}, f32[768,768]{1,0:T(8,128)})) %all-reduce.4.cloned.1.call-update) | async-done | bytes 9437200 | tf_op jit(solution)/shard_map/psum | solution.py:292
  (489 shorter events, 197.2 us)
Async XLA Ops:
  7.2 533.4 %copy-start = (bf16[768,768]{1,0:T(8,128)(2,1)S(1)}, bf16[768,768]{1,0:T(8,128)(2,1)}, u32[]{:S(2)}) copy-start(bf16[768,768]{1,0:T(8,128)(2,1)} %param.25) | copy-start | bytes 3538948
  7.2 143.1 %all-gather.4.cloned.1.call-start = ((), (), s32[]{:S(2)}) async-start(), calls=%async_computation.7 | async-start | bytes 15728640 | tf_op jit(solution)/shard_map/all_gather | solution.py:64
  25.1 528.9 %all-gather.6.cloned.1.call-start = ((), (), s32[]{:S(2)}) async-start(), calls=%async_computation.8 | async-start | bytes 11796480 | tf_op jit(solution)/shard_map/all_gather | solution.py:138
  25.9 617.2 %all-gather.8.cloned.1.call-start = ((), (), s32[]{:S(2)}) async-start(), calls=%async_computation.9 | async-start | bytes 11796480 | tf_op jit(solution)/shard_map/all_gather | solution.py:139
  26.6 39.5 %copy-start.65 = (s32[512]{0:T(512)}, s32[512]{0:T(512)S(1)}, u32[]{:S(2)}) copy-start(s32[512]{0:T(512)S(1)} %iota_add_fusion) | copy-start | bytes 6148
  30.1 36.1 %slice-start = ((bf16[1024,2304]{1,0:T(8,128)(2,1)}), bf16[1024,768]{1,0:T(8,128)(2,1)S(1)}, s32[]{:S(2)}) async-start(bf16[1024,2304]{1,0:T(8,128)(2,1)} %copy-done.18), calls=%async_computation.14 | async-start | bytes 3145728 | tf_op jit(solution)/shard_map/slice | solution.py:62
  545.3 115.1 %copy-start.11 = (bf16[1024,768]{1,0:T(8,128)(2,1)}, bf16[1024,768]{1,0:T(8,128)(2,1)S(1)}, u32[]{:S(2)}) copy-start(bf16[1024,768]{1,0:T(8,128)(2,1)S(1)} %multiply_convert_fusion.2) | copy-start | bytes 4718596
  549.1 51.1 %all-to-all-start = ((bf16[8,2,80,768]{3,2,1,0:T(8,128)(2,1)}), bf16[8,2,80,768]{3,2,1,0:T(8,128)(2,1)}, u32[]{:S(2)}, u32[]{:S(2)}) async-start(bf16[8,2,80,768]{3,2,1,0:T(8,128)(2,1)} %bitcast.332), calls=%async_computation | async-start | bytes 3932160 | tf_op jit(solution)/shard_map/all_to_all | solution.py:141
  655.8 50.8 %all-to-all-start.1 = ((bf16[8,2,80,768]{3,2,1,0:T(8,128)(2,1)}), bf16[8,2,80,768]{3,2,1,0:T(8,128)(2,1)}, u32[]{:S(2)}, u32[]{:S(2)}) async-start(bf16[8,2,80,768]{3,2,1,0:T(8,128)(2,1)} %copy.47), calls=%async_computation.1 | async-start | bytes 3932160 | tf_op jit(solution)/shard_map/all_to_all | solution.py:145
  660.9 193.9 %copy-start.23 = (f32[1024,16]{0,1:T(8,128)}, f32[1024,16]{0,1:T(8,128)S(1)}, u32[]{:S(2)}) copy-start(f32[1024,16]{0,1:T(8,128)S(1)} %get-tuple-element.1449) | copy-start | bytes 196612
  661.0 193.9 %copy-start.42 = (f32[1024]{0:T(1024)}, f32[1024]{0:T(1024)S(1)}, u32[]{:S(2)}) copy-start(f32[1024]{0:T(1024)S(1)} %get-tuple-element.1448) | copy-start | bytes 12292
  661.0 193.9 %copy-start.53 = (f32[1024]{0:T(1024)}, f32[1024]{0:T(1024)S(1)}, u32[]{:S(2)}) copy-start(f32[1024]{0:T(1024)S(1)} %fusion.138) | copy-start | bytes 12292
  712.8 142.0 %copy-start.57 = (f32[1024]{0:T(1024)}, f32[1024]{0:T(1024)S(1)}, u32[]{:S(2)}) copy-start(f32[1024]{0:T(1024)S(1)} %get-tuple-element.1446) | copy-start | bytes 12292
  712.9 142.0 %copy-start.59 = (f32[1024]{0:T(1024)}, f32[1024]{0:T(1024)S(1)}, u32[]{:S(2)}) copy-start(f32[1024]{0:T(1024)S(1)} %get-tuple-element.1063) | copy-start | bytes 12292
  717.0 50.2 %all-to-all-start.2 = ((bf16[8,2,80,768]{3,2,1,0:T(8,128)(2,1)}), bf16[8,2,80,768]{3,2,1,0:T(8,128)(2,1)S(1)}, u32[]{:S(2)}, u32[]{:S(2)}) async-start(bf16[8,2,80,768]{3,2,1,0:T(8,128)(2,1)} %bitcast.331), calls=%async_computation.2 | async-start | bytes 3932160 | tf_op jit(solution)/shard_map/all_to_all | solution.py:160
  767.2 22.5 %copy-start.21 = (bf16[8,2,80,768]{3,2,1,0:T(8,128)(2,1)}, bf16[8,2,80,768]{3,2,1,0:T(8,128)(2,1)S(1)}, u32[]{:S(2)}) copy-start(bf16[8,2,80,768]{3,2,1,0:T(8,128)(2,1)S(1)} %all-to-all-done.2) | copy-start | bytes 5898244
  802.6 49.8 %all-to-all-start.3 = ((bf16[8,2,80,768]{3,2,1,0:T(8,128)(2,1)}), bf16[8,2,80,768]{3,2,1,0:T(8,128)(2,1)S(1)}, u32[]{:S(2)}, u32[]{:S(2)}) async-start(bf16[8,2,80,768]{3,2,1,0:T(8,128)(2,1)} %copy.49), calls=%async_computation.3 | async-start | bytes 3932160 | tf_op jit(solution)/shard_map/all_to_all | solution.py:191
  806.2 907.1 %reduce-scatter.4.cloned.1.call-start = ((), (), s32[]{:S(2)}) async-start(), calls=%async_computation.10 | async-start | bytes 15728640 | tf_op jit(solution)/shard_map/reduce_scatter | solution.py:273
  1042.8 40.1 %copy-start.4 = (bf16[1,512,768]{1,2,0:T(8,128)(2,1)S(1)}, bf16[1,512,768]{1,2,0:T(8,128)(2,1)}, u32[]{:S(2)}) copy-start(bf16[1,512,768]{1,2,0:T(8,128)(2,1)} %copy-done.3) | copy-start | bytes 2359300 | tf_op jit(solution)/shard_map/while
  1167.5 30.2 %copy-start.71 = (f32[32,12]{0,1:T(8,128)S(1)}, f32[32,12]{0,1:T(8,128)}, u32[]{:S(2)}) copy-start(f32[32,12]{0,1:T(8,128)} %get-tuple-element.2625) | copy-start | bytes 4612 | tf_op jit(solution)/shard_map/while
  1197.6 22.3 %copy-start.16 = (bf16[2,512,768]{2,1,0:T(8,128)(2,1)S(1)}, bf16[2,512,768]{2,1,0:T(8,128)(2,1)}, u32[]{:S(2)}) copy-start(bf16[2,512,768]{2,1,0:T(8,128)(2,1)} %copy-done.15) | copy-start | bytes 4718596 | tf_op jit(solution)/shard_map/while
  1231.5 21.5 %copy-start.91 = (f32[12]{0:T(128)S(1)}, f32[12]{0:T(128)}, u32[]{:S(2)}) copy-start(f32[12]{0:T(128)} %get-tuple-element.2762) | copy-start | bytes 148 | tf_op jit(solution)/shard_map/while
  1231.5 21.5 %copy-start.93 = (f32[12]{0:T(128)S(1)}, f32[12]{0:T(128)}, u32[]{:S(2)}) copy-start(f32[12]{0:T(128)} %get-tuple-element.2764) | copy-start | bytes 148 | tf_op jit(solution)/shard_map/while
  1231.5 21.5 %copy-start.95 = (f32[12]{0:T(128)S(1)}, f32[12]{0:T(128)}, u32[]{:S(2)}) copy-start(f32[12]{0:T(128)} %get-tuple-element.2766) | copy-start | bytes 148 | tf_op jit(solution)/shard_map/while
  1231.5 21.5 %copy-start.97 = (f32[12]{0:T(128)S(1)}, f32[12]{0:T(128)}, u32[]{:S(2)}) copy-start(f32[12]{0:T(128)} %get-tuple-element.2768) | copy-start | bytes 148 | tf_op jit(solution)/shard_map/while
  1231.5 21.5 %copy-start.99 = (f32[12]{0:T(128)S(1)}, f32[12]{0:T(128)}, u32[]{:S(2)}) copy-start(f32[12]{0:T(128)} %get-tuple-element.2710) | copy-start | bytes 148 | tf_op jit(solution)/shard_map/while
  1231.5 21.5 %copy-start.101 = (f32[12]{0:T(128)S(1)}, f32[12]{0:T(128)}, u32[]{:S(2)}) copy-start(f32[12]{0:T(128)} %get-tuple-element.2712) | copy-start | bytes 148 | tf_op jit(solution)/shard_map/while
  1231.5 21.5 %copy-start.103 = (f32[12]{0:T(128)S(1)}, f32[12]{0:T(128)}, u32[]{:S(2)}) copy-start(f32[12]{0:T(128)} %get-tuple-element.2772) | copy-start | bytes 148 | tf_op jit(solution)/shard_map/while
  1231.5 21.5 %copy-start.105 = (f32[12]{0:T(128)S(1)}, f32[12]{0:T(128)}, u32[]{:S(2)}) copy-start(f32[12]{0:T(128)} %get-tuple-element.2714) | copy-start | bytes 148 | tf_op jit(solution)/shard_map/while
  1231.5 21.5 %copy-start.107 = (f32[12]{0:T(128)S(1)}, f32[12]{0:T(128)}, u32[]{:S(2)}) copy-start(f32[12]{0:T(128)} %get-tuple-element.2716) | copy-start | bytes 148 | tf_op jit(solution)/shard_map/while
  1231.5 21.5 %copy-start.109 = (f32[12]{0:T(128)S(1)}, f32[12]{0:T(128)}, u32[]{:S(2)}) copy-start(f32[12]{0:T(128)} %get-tuple-element.2718) | copy-start | bytes 148 | tf_op jit(solution)/shard_map/while
  1231.6 21.5 %copy-start.111 = (f32[12]{0:T(128)S(1)}, f32[12]{0:T(128)}, u32[]{:S(2)}) copy-start(f32[12]{0:T(128)} %get-tuple-element.2720) | copy-start | bytes 148 | tf_op jit(solution)/shard_map/while
  1231.6 21.5 %copy-start.113 = (f32[12]{0:T(128)S(1)}, f32[12]{0:T(128)}, u32[]{:S(2)}) copy-start(f32[12]{0:T(128)} %get-tuple-element.2722) | copy-start | bytes 148 | tf_op jit(solution)/shard_map/while
  1231.6 21.5 %copy-start.115 = (f32[12]{0:T(128)S(1)}, f32[12]{0:T(128)}, u32[]{:S(2)}) copy-start(f32[12]{0:T(128)} %get-tuple-element.2724) | copy-start | bytes 148 | tf_op jit(solution)/shard_map/while
  1231.6 21.5 %copy-start.117 = (f32[12]{0:T(128)S(1)}, f32[12]{0:T(128)}, u32[]{:S(2)}) copy-start(f32[12]{0:T(128)} %get-tuple-element.2726) | copy-start | bytes 148 | tf_op jit(solution)/shard_map/while
  1231.6 21.5 %copy-start.119 = (f32[12]{0:T(128)S(1)}, f32[12]{0:T(128)}, u32[]{:S(2)}) copy-start(f32[12]{0:T(128)} %get-tuple-element.2728) | copy-start | bytes 148 | tf_op jit(solution)/shard_map/while
  1231.6 21.5 %copy-start.121 = (f32[12]{0:T(128)S(1)}, f32[12]{0:T(128)}, u32[]{:S(2)}) copy-start(f32[12]{0:T(128)} %get-tuple-element.2730) | copy-start | bytes 148 | tf_op jit(solution)/shard_map/while
  1410.7 40.1 %copy-start.4 = (bf16[1,512,768]{1,2,0:T(8,128)(2,1)S(1)}, bf16[1,512,768]{1,2,0:T(8,128)(2,1)}, u32[]{:S(2)}) copy-start(bf16[1,512,768]{1,2,0:T(8,128)(2,1)} %copy-done.3) | copy-start | bytes 2359300 | tf_op jit(solution)/shard_map/while
  1535.3 30.2 %copy-start.71 = (f32[32,12]{0,1:T(8,128)S(1)}, f32[32,12]{0,1:T(8,128)}, u32[]{:S(2)}) copy-start(f32[32,12]{0,1:T(8,128)} %get-tuple-element.2625) | copy-start | bytes 4612 | tf_op jit(solution)/shard_map/while
  1565.5 22.5 %copy-start.16 = (bf16[2,512,768]{2,1,0:T(8,128)(2,1)S(1)}, bf16[2,512,768]{2,1,0:T(8,128)(2,1)}, u32[]{:S(2)}) copy-start(bf16[2,512,768]{2,1,0:T(8,128)(2,1)} %copy-done.15) | copy-start | bytes 4718596 | tf_op jit(solution)/shard_map/while
  1594.4 216.8 %reduce-scatter.6.cloned.1.call-start = ((), (), s32[]{:S(2)}) async-start(), calls=%async_computation.11 | async-start | bytes 11796480 | tf_op jit(solution)/shard_map/reduce_scatter | solution.py:184
  1607.2 302.0 %reduce-scatter.8.cloned.1.call-start = ((), (), s32[]{:S(2)}) async-start(), calls=%async_computation.12 | async-start | bytes 11796480 | tf_op jit(solution)/shard_map/reduce_scatter | solution.py:187
  1624.3 88.9 %copy-start.28 = (bf16[1024,768]{1,0:T(8,128)(2,1)S(1)}, bf16[1024,768]{1,0:T(8,128)(2,1)}, u32[]{:S(2)}) copy-start(bf16[1024,768]{1,0:T(8,128)(2,1)} %copy-done.27) | copy-start | bytes 4718596
  1624.3 483.7 %all-reduce.4.cloned.1.call-start = ((), (), s32[]{:S(2)}) async-start(), calls=%async_computation.13 | async-start | bytes 18874368 | tf_op jit(solution)/shard_map/psum | solution.py:292
  1723.9 189.7 %copy-start.13 = (bf16[2,512,768]{2,1,0:T(8,128)(2,1)S(1)}, bf16[2,512,768]{2,1,0:T(8,128)(2,1)}, u32[]{:S(2)}) copy-start(bf16[2,512,768]{2,1,0:T(8,128)(2,1)} %param.18) | copy-start | bytes 4718596
  1723.9 189.7 %copy-start.62 = (f32[1024]{0:T(1024)S(1)}, f32[1024]{0:T(1024)}, u32[]{:S(2)}) copy-start(f32[1024]{0:T(1024)} %copy-done.61) | copy-start | bytes 12292
  1723.9 189.7 %copy-start.67 = (f32[768]{0:T(1024)S(1)}, f32[768]{0:T(1024)}, u32[]{:S(2)}) copy-start(f32[768]{0:T(1024)} %param.21) | copy-start | bytes 9220
  1914.1 49.7 %copy-start.64 = (f32[1,4,2,128]{3,1,2,0:T(4,128)S(1)}, f32[1,4,2,128]{3,1,2,0:T(4,128)}, u32[]{:S(2)}) copy-start(f32[1,4,2,128]{3,1,2,0:T(4,128)} %copy-done.63) | copy-start | bytes 12292
  (150 other events, 1352.3 us)
Sparse Core Ops, SparseCore 0:
  25.3 125.0 all-gather.3
  152.2 96.3 all-gather.5
  250.4 96.3 all-gather.7
  1594.5 118.6 reduce-scatter.3
  1716.2 94.9 reduce-scatter.5
  1814.2 95.0 reduce-scatter.7
  1915.7 192.2 all-reduce.3
where the time goes:
time: 2130 us; the launch traced here: 2120 us
  matrix products  952 us (45%)
  waiting for transfers between devices  641 us (30%)
  local copies, waits for them, and re-layouts  224 us (11%)
  other arithmetic  206 us (10%)
  blocking collectives  42.5 us (2%)
  loops' own time  24.1 us (1%)
    dot_general x4, matrix products, score_block(): jnp.einsum('qhd,khd->hqk', query_heads, key_heads, preferred_element_type...  572 us
    psum x1, waiting for transfers between devices, on_device(): lax.psum((grad_joined_weight, grad_out_weight, grad_router, grad_table, g...  139 us
    while x184, local copies, waits for them, and re-layouts  106 us
    reduce_scatter x1, waiting for transfers between devices, on_device(): lax.psum_scatter(grad_expert_out.astype(jnp.bfloat16), 'narrow', scatter_...  93.8 us
    reduce_scatter x1, waiting for transfers between devices, on_device(): lax.psum_scatter(grad_expert_in.astype(jnp.bfloat16), 'narrow', scatter_d...  87.3 us
    reduce_scatter x1, waiting for transfers between devices, on_device(): lax.psum_scatter(grad_pairs.astype(jnp.bfloat16), 'narrow', scatter_dimen...  83.5 us
    all_gather x1, waiting for transfers between devices, on_device(): all_pairs = lax.all_gather(own_pairs, 'narrow', axis=1, tiled=True)  82.6 us
    convert_element_type x2, other arithmetic, attend_backward(): grad_scores = grad_scores.astype(jnp.bfloat16)  80.2 us
  transfers between devices with their start and end apart: 11, of which 9 were waited for; matrix products, arithmetic and copies ran while one was open for 26% of the time, Pallas kernels for 0%

commit v1 on v0

v1 whole, which is shorter than its diff:
```python
import jax
import jax.numpy as jnp
from jax import lax
from jax.experimental import pallas as pl
from jax.experimental.pallas import tpu as pltpu
from jax.sharding import PartitionSpec as P

epsilon = 1e-06
bucket_edges = (1, 2, 3, 4, 5, 6, 7, 8, 12, 16, 23, 32, 46, 64, 91)
LOG2E = 1.4426950408889634
LN2 = 0.6931471805599453
TILE = 128
VMEM_LIMIT = 56 * 1024 * 1024
NT = (((1,), (1,)), ((), ()))
NN = (((1,), (0,)), ((), ()))
TN = (((0,), (0,)), ((), ()))
BF16 = jnp.bfloat16
F32 = jnp.float32


def dotf(a, b, dims=NN):
    return lax.dot_general(a, b, dims, preferred_element_type=F32)


def rms_factor(values):
    return lax.rsqrt(jnp.mean(values * values, axis=-1, keepdims=True) + epsilon)


def rms_pull(values, factor, gain, grad):
    normal = values * factor
    scaled = grad * gain
    mean = jnp.mean(scaled * normal, axis=-1, keepdims=True)
    return (scaled - normal * mean) * factor, grad * normal


def bucket_of(offsets, bucket_count):
    magnitude = jnp.abs(offsets)
    bucket = jnp.zeros_like(offsets)
    for border in bucket_edges:
        bucket = bucket + (magnitude >= border).astype(jnp.int32)
    return bucket + bucket_count // 2 * (offsets > 0).astype(jnp.int32)


def pieces(x):
    hi = x.astype(BF16)
    rest = x - hi.astype(F32)
    mid = rest.astype(BF16)
    low = (rest - mid.astype(F32)).astype(BF16)
    return hi, mid, low


def bias_tiles(bias_table):
    buckets, heads = bias_table.shape
    place = jnp.arange(TILE, dtype=jnp.int32)
    shift = jnp.arange(-1, 2, dtype=jnp.int32) * TILE
    offsets = shift[:, None, None] + place[None, :, None] - place[None, None, :]
    bucket = bucket_of(offsets, buckets)[None]
    table = bias_table.T * LOG2E
    tiles = jnp.zeros((heads, 3, TILE, TILE), F32)
    for row in range(buckets):
        tiles = jnp.where(bucket == row, table[:, row][:, None, None, None], tiles)
    left = tiles[:, :1] - table[:, buckets // 2 - 1][:, None, None, None]
    right = tiles[:, 2:] - table[:, buckets - 1][:, None, None, None]
    return jnp.concatenate((tiles, left, right), axis=1)


def query_lanes(bias_table, rows):
    buckets, heads = bias_table.shape
    count = rows // TILE
    left = pieces(bias_table[buckets // 2 - 1] * LOG2E)
    right = pieces(bias_table[buckets - 1] * LOG2E)
    one, zero = jnp.ones((heads,), BF16), jnp.zeros((heads,), BF16)
    blocks = []
    for a in range(count):
        lanes = [zero] * 3 + list(left) + list(right)
        for t in range(count):
            lanes += list(left) if t <= a - 2 else list(right) if t >= a + 2 else [zero] * 3
        lanes += [one]
        lanes += [zero] * (64 - len(lanes))
        blocks.append(jnp.stack(lanes + lanes, axis=1))
    pattern = jnp.stack(blocks, axis=1)
    return jnp.broadcast_to(pattern[:, :, None, :], (heads, count, TILE, 128)).reshape(
        heads, rows, 128
    )


def key_lanes(me, lengths, rows):
    count = rows // TILE
    lane = (jnp.arange(128, dtype=jnp.int32) % 64)[None, :]
    place = jnp.arange(rows, dtype=jnp.int32)
    out = []
    for u in range(4):
        block = me ^ u
        base = lane < 3
        base = base | ((lane >= 3) & (lane < 6) & (block < me))
        base = base | ((lane >= 6) & (lane < 9) & (block > me))
        if u == 0:
            for t in range(count):
                own = (place // TILE == t)[:, None]
                base = base | ((lane >= 9 + 3 * t) & (lane < 12 + 3 * t) & own)
        base = jnp.broadcast_to(base, (rows, 128)).astype(F32)
        dead = (block * rows + place)[None, :] >= lengths[:, None]
        masked = (lane == 9 + 3 * count)[None] & dead[:, :, None]
        out.append(jnp.where(masked, -1e30, base[None]).astype(BF16))
    return jnp.stack(out, axis=1)


def neighbour_flags(me):
    one, three = me ^ 1, me ^ 3
    return jnp.stack((one == me + 1, one == me - 1, three == me + 1, three == me - 1)).astype(F32)


def own_lanes(head, rows):
    lane = lax.broadcasted_iota(jnp.int32, (rows, 128), 1)
    return (lane < 64) if head == 0 else (lane >= 64)


def forward_kernel(flags, q, kv, klanes, qlanes, tiles, att, qaug, s_ref):
    rows = q.shape[1]
    count = rows // TILE
    one = jnp.ones((), BF16)
    outs = []
    for h in range(2):
        own = own_lanes(h, rows)
        qa = jnp.where(own, q[0], qlanes[h])
        for u in range(4):
            ka = jnp.where(own, kv[0, u, :, :128], klanes[0, u])
            start = u * rows
            s_ref[h, :, start : start + rows] = dotf(qa, ka, NT)
            if u == 0:
                for a in range(count):
                    for t in range(max(0, a - 1), min(count, a + 2)):
                        spot = (h, slice(a * 128, a * 128 + 128), slice(t * 128, t * 128 + 128))
                        s_ref[spot] = s_ref[spot] + tiles[h, t - a + 1].T
            if u in (1, 3):
                spot = (h, slice(rows - 128, rows), slice(start, start + 128))
                s_ref[spot] = s_ref[spot] + tiles[h, 4].T * flags[u - 1]
                spot = (h, slice(0, 128), slice(start + rows - 128, start + rows))
                s_ref[spot] = s_ref[spot] + tiles[h, 3].T * flags[u]
        top = jnp.max(s_ref[h], axis=1, keepdims=True)
        total = None
        for u in range(4):
            weights = jnp.exp2(s_ref[h, :, u * rows : (u + 1) * rows] - top).astype(BF16)
            part = dotf(weights, jnp.where(own, kv[0, u, :, 128:], one))
            total = part if total is None else total + part
        turned = pltpu.roll(total, 64, 1)
        outs.append(total / turned)
        hi, mid, low = pieces(top + jnp.log2(jnp.where(own, turned, total)))
        lane = lax.broadcasted_iota(jnp.int32, (rows, 128), 1) - (64 if h == 0 else 0)
        qaug[0, h] = jnp.where(
            lane == 0, -hi, jnp.where(lane == 1, -mid, jnp.where(lane == 2, -low, qa))
        )
    att[0] = jnp.where(own_lanes(0, rows), outs[0], outs[1]).astype(BF16)


def attend_forward(flags, q, kv, klanes, qlanes, tiles):
    seqs, rows, width = q.shape
    pairs = width // 128
    heads_block = pl.BlockSpec((1, rows, 128), lambda s, p: (s, 0, p))
    return pl.pallas_call(
        forward_kernel,
        grid=(seqs, pairs),
        in_specs=[
            pl.BlockSpec(memory_space=pltpu.SMEM),
            heads_block,
            pl.BlockSpec((1, 4, rows, 256), lambda s, p: (s, 0, 0, p)),
            pl.BlockSpec((1, 4, rows, 128), lambda s, p: (s, 0, 0, 0)),
            pl.BlockSpec((2, rows, 128), lambda s, p: (p, 0, 0)),
            pl.BlockSpec((2, 5, TILE, TILE), lambda s, p: (p, 0, 0, 0)),
        ],
        out_specs=[heads_block, pl.BlockSpec((1, 2, rows, 128), lambda s, p: (s, p, 0, 0))],
        out_shape=[
            jax.ShapeDtypeStruct((seqs, rows, width), BF16),
            jax.ShapeDtypeStruct((seqs, 2 * pairs, rows, 128), BF16),
        ],
        scratch_shapes=[pltpu.VMEM((2, rows, 4 * rows), F32)],
        compiler_params=pltpu.CompilerParams(
            dimension_semantics=("arbitrary", "arbitrary"), vmem_limit_bytes=VMEM_LIMIT
        ),
        cost_estimate=pl.CostEstimate(
            flops=seqs * 16 * rows * rows * 128 * 2 * pairs,
            bytes_accessed=seqs * rows * width * 24,
            transcendentals=seqs * 8 * pairs * rows * rows,
        ),
        name="attend_forward",
    )(flags, q, kv, klanes, qlanes, tiles)


def backward_kernel(flags, qaug, kv, att, do, klanes, tiles, dq, dkv, table):
    rows = do.shape[1]
    count = rows // TILE
    own0 = own_lanes(0, rows)
    prod = do[0].astype(F32) * att[0].astype(F32)
    one, zero = jnp.ones((), BF16), jnp.zeros((), BF16)
    turned = []
    for h in range(2):
        own = own_lanes(h, rows)
        qa = qaug[0, h]
        delta = jnp.sum(jnp.where(own, prod, 0.0), axis=1, keepdims=True)
        hi, mid, _ = pieces(jnp.broadcast_to(delta, (rows, 128)))
        lane = lax.broadcasted_iota(jnp.int32, (rows, 128), 1) - (64 if h == 0 else 0)
        doa = jnp.where(own, do[0], jnp.where(lane == 0, -hi, jnp.where(lane == 1, -mid, zero)))
        near = {}
        corner = {-1: None, 1: None}
        dqt = None
        for u in range(4):
            ka = jnp.where(own, kv[0, u, :, :128], klanes[0, u])
            va = jnp.where(own, kv[0, u, :, 128:], one)
            st = dotf(ka, qa, NT)
            if u == 0:
                strips = []
                for t in range(count):
                    row = []
                    for a in range(count):
                        x = st[t * 128 : t * 128 + 128, a * 128 : a * 128 + 128]
                        row.append(x + tiles[h, t - a + 1] if abs(t - a) <= 1 else x)
                    strips.append(jnp.concatenate(row, axis=1))
                st = jnp.concatenate(strips, axis=0)
            if u in (1, 3):
                after, before = flags[u - 1], flags[u]
                first = jnp.concatenate(
                    (st[:128, : rows - 128], st[:128, rows - 128 :] + tiles[h, 4] * after), axis=1
                )
                last = jnp.concatenate(
                    (st[rows - 128 :, :128] + tiles[h, 3] * before, st[rows - 128 :, 128:]), axis=1
                )
                st = jnp.concatenate((first, st[128 : rows - 128], last), axis=0)
            probs = jnp.exp2(st)
            ds = probs * dotf(va, doa, NT)
            probs_low, ds_low = probs.astype(BF16), ds.astype(BF16)
            if u == 0:
                for d in (-1, 0, 1):
                    for a in range(max(0, -d), min(count, count - d)):
                        t = a + d
                        x = ds[t * 128 : t * 128 + 128, a * 128 : a * 128 + 128]
                        near[d] = near[d] + x if d in near else x
            if u in (1, 3):
                for d, x in ((1, ds[:128, rows - 128 :] * after), (-1, ds[rows - 128 :, :128] * before)):
                    corner[d] = x if corner[d] is None else corner[d] + x
            dv = dotf(probs_low, doa).astype(BF16)
            dk = (dotf(ds_low, qa) * LN2).astype(BF16)
            if h == 0:
                dkv[0, u, :, :128], dkv[0, u, :, 128:] = dk, dv
            else:
                dkv[0, u, :, :128] = jnp.where(own0, dkv[0, u, :, :128], dk)
                dkv[0, u, :, 128:] = jnp.where(own0, dkv[0, u, :, 128:], dv)
            part = dotf(ka.T, ds_low)
            dqt = part if dqt is None else dqt + part
        turned.append(dqt.T)
        group = lax.broadcasted_iota(jnp.int32, (TILE, TILE), 0) // 8 * 8
        upper = lax.broadcasted_iota(jnp.int32, (TILE, TILE), 1) >= group
        before, after = near[-1] + corner[-1], near[1] + corner[1]
        inner = (jnp.where(upper, near[0], before), jnp.where(upper, after, near[0]))
        for i, x in enumerate(inner):
            lined = x[:8]
            for g in range(1, TILE // 8):
                lined = lined + pltpu.roll(x[8 * g : 8 * g + 8], TILE - 8 * g, 1)
            table[0, h, 8 * i : 8 * i + 8, :] = lined
        outer = (jnp.where(upper, before, 0.0), jnp.where(upper, 0.0, after), corner[-1], corner[1])
        for i, x in enumerate(outer):
            table[0, h, 16 + i : 17 + i, :] = jnp.sum(x, axis=0, keepdims=True)
    dq[0] = (jnp.where(own0, turned[0], turned[1]) * 0.125).astype(BF16)
    for h in range(2):
        for a in range(count):
            rest = jnp.sum(turned[h][a * 128 : a * 128 + 128], axis=0, keepdims=True)
            table[0, h, 20 + a : 21 + a, :] = rest


def attend_backward(flags, qaug, kv, att, do, klanes, tiles):
    seqs, rows, width = do.shape
    pairs = width // 128
    heads_block = pl.BlockSpec((1, rows, 128), lambda s, p: (s, 0, p))
    pair_block = pl.BlockSpec((1, 4, rows, 256), lambda s, p: (s, 0, 0, p))
    return pl.pallas_call(
        backward_kernel,
        grid=(seqs, pairs),
        in_specs=[
            pl.BlockSpec(memory_space=pltpu.SMEM),
            pl.BlockSpec((1, 2, rows, 128), lambda s, p: (s, p, 0, 0)),
            pair_block,
            heads_block,
            heads_block,
            pl.BlockSpec((1, 4, rows, 128), lambda s, p: (s, 0, 0, 0)),
            pl.BlockSpec((2, 5, TILE, TILE), lambda s, p: (p, 0, 0, 0)),
        ],
        out_specs=[
            heads_block,
            pair_block,
            pl.BlockSpec((1, 2, 32, 128), lambda s, p: (s, p, 0, 0)),
        ],
        out_shape=[
            jax.ShapeDtypeStruct((seqs, rows, width), BF16),
            jax.ShapeDtypeStruct((seqs, 4, rows, 2 * width), BF16),
            jax.ShapeDtypeStruct((seqs, 2 * pairs, 32, 128), F32),
        ],
        compiler_params=pltpu.CompilerParams(
            dimension_semantics=("arbitrary", "arbitrary"), vmem_limit_bytes=VMEM_LIMIT
        ),
        cost_estimate=pl.CostEstimate(
            flops=seqs * 40 * rows * rows * 128 * 2 * pairs,
            bytes_accessed=seqs * rows * width * 40,
            transcendentals=seqs * 8 * pairs * rows * rows,
        ),
        name="attend_backward",
    )(flags, qaug, kv, att, do, klanes, tiles)


def table_grad(table, rows, bucket_count):
    count = rows // TILE
    heads = table.shape[0]
    row = jnp.arange(16, dtype=jnp.int32)[:, None]
    lane = jnp.arange(TILE, dtype=jnp.int32)[None, :]
    bucket = bucket_of(row // 8 * TILE + row % 8 - lane, bucket_count)
    ids = jnp.arange(bucket_count, dtype=jnp.int32)
    onehot = (bucket[None] == ids[:, None, None]).astype(F32)
    near = jnp.einsum("hil,bil->bh", table[:, :16], onehot, precision=lax.Precision.HIGHEST)
    halves = table[:, 20 : 20 + count].reshape(heads // 2, 2, count, 2, 64)
    rest = jnp.stack((halves[:, 0, :, 1], halves[:, 1, :, 0]), axis=1).reshape(heads, count, 64)
    outer = jnp.sum(table[:, 16:20], axis=2)
    left = jnp.sum(rest[:, :, 3], axis=1) + outer[:, 0] - outer[:, 2]
    right = jnp.sum(rest[:, :, 6], axis=1) + outer[:, 1] - outer[:, 3]
    for a in range(count):
        for t in range(count):
            if t <= a - 2:
                left = left + rest[:, a, 9 + 3 * t]
            if t >= a + 2:
                right = right + rest[:, a, 9 + 3 * t]
    far = jnp.where((ids == bucket_count // 2 - 1)[:, None], left[None, :], 0.0)
    return near + far + jnp.where((ids == bucket_count - 1)[:, None], right[None, :], 0.0)


def expert_kernel(own, x, c, units, w_in, w_out, router, hidden, grad_pre, low_c, back, grad_x,
                  grad_logits, gate_ref, probs_ref, out_acc, x_acc):
    step = pl.program_id(0)
    rows = x.shape[0]
    chunk = TILE

    @pl.when(step == 0)
    def _():
        logits = dotf(x[...], router[...])
        weights = jnp.exp(logits - jnp.max(logits, axis=1, keepdims=True))
        probs = weights / jnp.sum(weights, axis=1, keepdims=True)
        probs_ref[...] = probs
        ids = lax.broadcasted_iota(jnp.int32, probs.shape, 1)
        gate = jnp.sum(jnp.where(ids == own[0], probs, 0.0), axis=1, keepdims=True)
        gate_ref[...] = jnp.broadcast_to(gate, gate_ref.shape)
        low_c[...] = (c[...].astype(F32) * gate).astype(BF16)
        out_acc[...] = jnp.zeros_like(out_acc)
        x_acc[...] = jnp.zeros_like(x_acc)

    for r in range(rows // chunk):
        part = slice(r * chunk, r * chunk + chunk)
        pre = dotf(x[part, :], w_in[0])
        below = 0.5 + 0.5 * lax.erf(pre * 0.7071067811865476)
        hid = (pre * below).astype(BF16)
        slope = below + pre * (jnp.exp(pre * pre * -0.5) * 0.3989422804014327)
        gate = gate_ref[part, :1]
        low = (slope * gate * units[part, :].astype(F32)).astype(BF16)
        hidden[part, :] = hid
        grad_pre[part, :] = low
        out_acc[part, :] += dotf(hid, w_out[0])
        x_acc[part, :] += dotf(low, w_in[0], NT)

    @pl.when(step == pl.num_programs(0) - 1)
    def _():
        result = out_acc[...]
        gate = gate_ref[:, :1]
        probs = probs_ref[...]
        grad_gate = jnp.sum(c[...].astype(F32) * result.astype(BF16).astype(F32), axis=1, keepdims=True)
        ids = lax.broadcasted_iota(jnp.int32, probs.shape, 1)
        mine = jnp.where(ids == own[0], 1.0, 0.0)
        low = (grad_gate * probs * (mine - gate)).astype(BF16)
        grad_logits[...] = low
        back[...] = (result * gate).astype(BF16)
        grad_x[...] = (x_acc[...] + dotf(low, router[...], NT)).astype(BF16)


def run_expert(own, index, x, c, units, w_in, w_out, router):
    rows, width = x.shape
    hid = w_in.shape[2]
    experts = router.shape[1]
    step = 768
    whole = lambda f: (0, 0)
    sliced = lambda f: (0, f)
    return pl.pallas_call(
        expert_kernel,
        grid=(hid // step,),
        in_specs=[
            pl.BlockSpec(memory_space=pltpu.SMEM),
            pl.BlockSpec((rows, width), whole),
            pl.BlockSpec((rows, width), whole),
            pl.BlockSpec((rows, step), sliced),
            pl.BlockSpec((1, width, step), lambda f: (index, 0, f)),
            pl.BlockSpec((1, step, width), lambda f: (index, f, 0)),
            pl.BlockSpec((width, experts), whole),
        ],
        out_specs=[
            pl.BlockSpec((rows, step), sliced),
            pl.BlockSpec((rows, step), sliced),
            pl.BlockSpec((rows, width), whole),
            pl.BlockSpec((rows, width), whole),
            pl.BlockSpec((rows, width), whole),
            pl.BlockSpec((rows, experts), whole),
        ],
        out_shape=[
            jax.ShapeDtypeStruct((rows, hid), BF16),
            jax.ShapeDtypeStruct((rows, hid), BF16),
            jax.ShapeDtypeStruct((rows, width), BF16),
            jax.ShapeDtypeStruct((rows, width), BF16),
            jax.ShapeDtypeStruct((rows, width), BF16),
            jax.ShapeDtypeStruct((rows, experts), BF16),
        ],
        scratch_shapes=[
            pltpu.VMEM((rows, 128), F32),
            pltpu.VMEM((rows, experts), F32),
            pltpu.VMEM((rows, width), F32),
            pltpu.VMEM((rows, width), F32),
        ],
        compiler_params=pltpu.CompilerParams(
            dimension_semantics=("arbitrary",), vmem_limit_bytes=VMEM_LIMIT
        ),
        cost_estimate=pl.CostEstimate(
            flops=6 * rows * width * hid,
            bytes_accessed=4 * width * hid + 6 * rows * hid,
            transcendentals=2 * rows * hid,
        ),
        name="run_expert",
    )(own, x, c, units, w_in, w_out, router)


def swap(x, bit):
    return lax.ppermute(x, "narrow", [(i, i ^ bit) for i in range(4)])


def gather_blocks(own):
    half = own.shape[0] // 2
    one, two = swap(own, 1), swap(own, 2)
    three = jnp.concatenate((swap(two[:half], 1), swap(one[half:], 2)), axis=0)
    return jnp.stack((own, one, two, three))


def scatter_blocks(blocks):
    half = blocks[0].shape[0] // 2
    low = [b.astype(BF16) for b in blocks]
    from_one = swap(low[3][:half], 1).astype(F32)
    from_two = swap(low[3][half:], 2).astype(F32)
    one = jnp.concatenate((blocks[1][:half], blocks[1][half:] + from_two), axis=0).astype(BF16)
    two = jnp.concatenate((blocks[2][:half] + from_one, blocks[2][half:]), axis=0).astype(BF16)
    return blocks[0] + swap(one, 1).astype(F32) + swap(two, 2).astype(F32)


def after(x, *others):
    return lax.optimization_barrier((x,) + others)[0]


def on_device(
    hidden_in,
    lengths,
    routes,
    norm_gain_attn,
    query_weight,
    key_weight,
    value_weight,
    out_weight,
    bias_table,
    norm_gain_ffn,
    router_weight,
    expert_in,
    expert_out,
    cotangent,
):
    wide_count = lax.axis_size("wide")
    seq_count, rows, width = hidden_in.shape
    bucket_count, head_count = bias_table.shape
    pairs = width // 128
    tokens = seq_count * rows
    local_experts = expert_in.shape[0]
    expert_count = local_experts * wide_count
    capacity = 5 * tokens // (4 * expert_count)
    slots = wide_count * capacity
    me = lax.axis_index("narrow")
    mine = lax.axis_index("wide") * local_experts

    source = hidden_in.astype(F32).reshape(tokens, width)
    factor_attn = rms_factor(source)
    normed = (source * factor_attn * norm_gain_attn).astype(BF16)
    normed_seqs = normed.reshape(seq_count, rows, width)
    pair_weight = jnp.stack(
        (key_weight.reshape(width, pairs, 128), value_weight.reshape(width, pairs, 128)), axis=2
    ).reshape(width, 2 * width)
    blocks = [gather_blocks(normed_seqs[s]) for s in range(seq_count)]
    expert_in, expert_out, _ = lax.optimization_barrier((expert_in, expert_out, blocks[-1]))
    whole_in = lax.all_gather(expert_in, "narrow", axis=2, tiled=True)
    whole_out = lax.all_gather(expert_out, "narrow", axis=1, tiled=True)

    queries = (dotf(normed, query_weight) * (LOG2E / 8)).astype(BF16).reshape(seq_count, rows, width)
    flags = neighbour_flags(me)
    klanes = key_lanes(me, lengths, rows)
    qlanes = query_lanes(bias_table, rows)
    tiles = bias_tiles(bias_table)

    route = routes.reshape(tokens)
    position = me * rows + jnp.arange(rows, dtype=jnp.int32)
    live = (position[None, :] < lengths[:, None]).reshape(tokens)
    expert_ids = jnp.arange(expert_count, dtype=jnp.int32)
    chosen = ((route[:, None] == expert_ids[None, :]) & live[:, None]).astype(F32)
    token_ids = jnp.arange(tokens, dtype=jnp.int32)
    earlier = (token_ids[:, None] > token_ids[None, :]).astype(BF16)
    place = jnp.sum(dotf(earlier, chosen.astype(BF16)) * chosen, axis=-1).astype(jnp.int32)
    kept = live & (place < capacity)
    slot = route // local_experts * capacity + place
    slot_ids = jnp.arange(slots, dtype=jnp.int32)
    maps, cots = [], []
    for e in range(local_experts):
        due = jnp.where(kept & (route % local_experts == e), slot, -1)
        maps.append((slot_ids[:, None] == due[None, :]).astype(BF16))

    def to_experts(values, e):
        sent = dotf(maps[e], values).astype(BF16).reshape(wide_count, capacity, width)
        return lax.all_to_all(sent, "wide", 0, 0, tiled=True).reshape(slots, width)

    def to_tokens(values, e):
        sent = values.reshape(wide_count, capacity, width)
        got = lax.all_to_all(sent, "wide", 0, 0, tiled=True).reshape(slots, width)
        return dotf(maps[e], got, TN)

    cot = cotangent.reshape(tokens, width)
    cots = [to_experts(cot, e) for e in range(local_experts)]

    kvs, atts, qaugs = [], [], []
    for s in range(seq_count):
        kv = dotf(blocks[s].reshape(4 * rows, width), pair_weight).astype(BF16)
        kvs.append(kv.reshape(1, 4, rows, 2 * width))
        att, qaug = attend_forward(flags, queries[s : s + 1], kvs[s], klanes[s : s + 1], qlanes, tiles)
        atts.append(att)
        qaugs.append(qaug)
    attended = jnp.concatenate(atts, axis=0).reshape(tokens, width)
    residual = source + dotf(attended, out_weight)
    factor_ffn = rms_factor(residual)
    ffn_input = (residual * factor_ffn * norm_gain_ffn).astype(BF16)

    xs = [to_experts(ffn_input, e) for e in range(local_experts)]
    units = [dotf(cots[e], whole_out[e], NT).astype(BF16) for e in range(local_experts)]
    results, grad_rows, grad_in, grad_out, grad_router = [], [], [], [], 0.0
    for e in range(local_experts):
        own = jnp.reshape(mine + e, (1,))
        hidden, grad_pre, low_c, back, grad_x, grad_logits = run_expert(
            own, e, xs[e], cots[e], units[e], whole_in, whole_out, router_weight
        )
        grad_rows.append(to_tokens(grad_x, e))
        results.append(back)
        grad_in.append(dotf(xs[e], grad_pre, TN).astype(BF16))
        grad_out.append(dotf(hidden, low_c, TN).astype(BF16))
        grad_router = grad_router + dotf(xs[e], grad_logits, TN)
    grad_expert_in = lax.psum_scatter(
        jnp.stack(grad_in), "narrow", scatter_dimension=2, tiled=True
    ).astype(F32)
    grad_expert_out = lax.psum_scatter(
        jnp.stack(grad_out), "narrow", scatter_dimension=1, tiled=True
    ).astype(F32)

    grad_ffn_input = sum(grad_rows)
    grad_top = cot.astype(F32)
    grad_norm, gain_ffn = rms_pull(residual, factor_ffn, norm_gain_ffn, grad_ffn_input)
    gain_ffn = jnp.sum(gain_ffn, axis=0)
    grad_residual = grad_top + grad_norm
    grad_branch = grad_residual.astype(BF16)
    grad_out_weight = dotf(attended, grad_branch, TN)
    grad_attended = dotf(grad_branch, out_weight, NT).astype(BF16).reshape(seq_count, rows, width)

    results = [to_tokens(after(results[e], grad_branch), e) for e in range(local_experts)]
    block_out = residual + sum(results)

    dqs, dkvs, tables = [], [], []
    for s in range(seq_count):
        dq, dkv, table = attend_backward(
            flags, qaugs[s], kvs[s], atts[s], grad_attended[s : s + 1], klanes[s : s + 1], tiles
        )
        dqs.append(dq)
        dkvs.append(dkv)
        tables.append(table)
    grad_table = table_grad(sum(tables)[0], rows, bucket_count)
    grad_queries = jnp.concatenate(dqs, axis=0).reshape(tokens, width)
    grad_pairs = jnp.concatenate(dkvs, axis=0)
    normed_all = jnp.stack(blocks)
    grad_q = dotf(normed, grad_queries, TN)
    grad_kv = dotf(
        normed_all.reshape(4 * tokens, width), grad_pairs.reshape(4 * tokens, 2 * width), TN
    )
    parts = []
    for s in range(seq_count):
        part = dotf(dkvs[s].reshape(4 * rows, 2 * width), pair_weight, NT).reshape(4, rows, width)
        parts.append(scatter_blocks([part[u] for u in range(4)]))
    grad_normed = jnp.concatenate(parts, axis=0) + dotf(grad_queries, query_weight, NT)
    grad_source, gain_attn = rms_pull(source, factor_attn, norm_gain_attn, grad_normed)
    gain_attn = jnp.sum(gain_attn, axis=0)
    grad_hidden = grad_residual + grad_source

    summed = lax.psum(
        (grad_q, grad_kv, grad_out_weight, grad_router, grad_table, gain_attn, gain_ffn),
        ("narrow", "wide"),
    )
    sum_kv = summed[1].reshape(width, pairs, 2, 128)
    out_shape = (seq_count, rows, width)
    return (
        block_out.reshape(out_shape),
        grad_hidden.reshape(out_shape),
        summed[5],
        summed[0],
        sum_kv[:, :, 0].reshape(width, width),
        sum_kv[:, :, 1].reshape(width, width),
        summed[2],
        summed[4],
        summed[6],
        summed[3],
        grad_expert_in,
        grad_expert_out,
    )


def solution(mesh):
    placed = (
        P("wide", "narrow", None),
        P("wide"),
        P("wide", "narrow", None),
        P(),
        P(),
        P(),
        P(),
        P(),
        P(),
        P(),
        P(),
        P("wide", None, "narrow"),
        P("wide", "narrow", None),
        P("wide", "narrow", None),
    )
    return jax.shard_map(
        on_device,
        mesh=mesh,
        in_specs=placed,
        out_specs=(
            P("wide", "narrow", None),
            P("wide", "narrow", None),
            P(),
            P(),
            P(),
            P(),
            P(),
            P(),
            P(),
            P(),
            P("wide", None, "narrow"),
            P("wide", "narrow", None),
        ),
        check_vma=False,
    )
```

time: 2130 us -> 883 us (0.41)
  matrix products: 952 us -> 148 us
  waiting for transfers between devices: 641 us -> 301 us
  Pallas kernels: 0 us -> 170 us
  local copies, waits for them, and re-layouts: 224 us -> 58.6 us
  other arithmetic: 206 us -> 77.2 us
  starting transfers between devices: 17.3 us -> 60.4 us
  loops' own time: 24.1 us -> 0 us
    dot_general x36 -> x29, matrix products: 952 us -> 148 us  [the longest x28 148 us: dotf(): return lax.dot_general(a, b, dims, preferred_element_type=F32)]
    pallas_call x0 -> x6, Pallas kernels: none -> 170 us  [the longest x2 71.4 us: attend_backward(): pl.pallas_call(backward_kernel, grid=(seqs, pairs), in_specs=[pl.BlockSpe...]
    psum x1, waiting for transfers between devices: 139 us -> 0.01 us  [on_device(): lax.psum((grad_q, grad_kv, grad_out_weight, grad_router, grad_table, gain...]
    all_to_all x4 -> x8, waiting for transfers between devices: 154 us -> 41.5 us  [the longest x4 20.9 us: to_experts(): return lax.all_to_all(sent, 'wide', 0, 0, tiled=True).reshape(slots, width)]
    while x184 -> x0, local copies, waits for them, and re-layouts: 106 us -> none
    reduce_scatter x3 -> x2, waiting for transfers between devices: 265 us -> 173 us  [the longest x1 94.1 us: on_device(): lax.psum_scatter(jnp.stack(grad_in), 'narrow', scatter_dimension=2, tiled...]
    convert_element_type x6 -> x11, other arithmetic: 90.9 us -> 13.5 us  [the longest x1 4.36 us: on_device(): grad_expert_in = lax.psum_scatter(jnp.stack(grad_in), 'narrow', scatter_d...]
    ppermute x0 -> x16, waiting for transfers between devices: none -> 70.4 us  [swap(): return lax.ppermute(x, 'narrow', [(i, i ^ bit) for i in range(4)])]
  transfers between devices with their start and end apart: 11 -> 29, of which waited for: 9 -> 15; matrix products, arithmetic and copies ran while one was open for 26% -> 25% of each run, Pallas kernels for 0% -> 11%
where the time goes in v1:
time: 883 us; the launch traced here: 876 us
  waiting for transfers between devices  301 us (34%)
  Pallas kernels  170 us (19%)
  matrix products  148 us (17%)
  other arithmetic  77.2 us (9%)
  starting transfers between devices  60.4 us (7%)
  local copies, waits for them, and re-layouts  58.6 us (7%)
  blocking collectives  45.7 us (5%)
  between operations  15 us (2%)
    dot_general x28, matrix products, dotf(): return lax.dot_general(a, b, dims, preferred_element_type=F32)  148 us
    reduce_scatter x1, waiting for transfers between devices, on_device(): lax.psum_scatter(jnp.stack(grad_in), 'narrow', scatter_dimension=2, tiled...  94.1 us
    reduce_scatter x1, waiting for transfers between devices, on_device(): lax.psum_scatter(jnp.stack(grad_out), 'narrow', scatter_dimension=1, tile...  78.5 us
    pallas_call x2, Pallas kernels, attend_backward(): pl.pallas_call(backward_kernel, grid=(seqs, pairs), in_specs=[pl.BlockSpe...  71.4 us
    ppermute x16, waiting for transfers between devices, swap(): return lax.ppermute(x, 'narrow', [(i, i ^ bit) for i in range(4)])  70.4 us
    pallas_call x2, Pallas kernels, attend_forward(): pl.pallas_call(forward_kernel, grid=(seqs, pairs), in_specs=[pl.BlockSpec...  52.6 us
    pallas_call x2, Pallas kernels, run_expert(): pl.pallas_call(expert_kernel, grid=(hid // step,), in_specs=[pl.BlockSpec...  46.1 us
    psum x1, blocking collectives, on_device(): lax.psum((grad_q, grad_kv, grad_out_weight, grad_router, grad_table, gain...  45.7 us
  transfers between devices with their start and end apart: 29, of which 15 were waited for; matrix products, arithmetic and copies ran while one was open for 25% of the time, Pallas kernels for 11%

profile of v1, /device:TPU:0, one launch (start us, length us, event | category | flops | bytes accessed | tf_op | source)
XLA Modules:
  0.0 876.4 jit_solution(11657472379469071447)
XLA Ops:
  17.8 16.0 %collective-permute-done.5 = bf16[512,768]{1,0:T(8,128)(2,1)S(1)} collective-permute-done((bf16[512,768]{1,0:T(8,128)(2,1)S(1)}, bf16[512,768]{1,0:T(8,128)(2,1)S(1)}, u32[]{:S(2)}, u32[]{:S(2)}) %collective-permute-start.5) | collective-permute-done | bytes 786464 | tf_op jit(solution)/shard_map/ppermute | solution.py:432
  37.3 7.0 collective-permute-done.6
  56.2 4.9 all-to-all-start.1
  74.4 9.2 %select_select_fusion = f32[12,3,128,128]{3,2,1,0:T(8,128)S(1)} fusion(f32[12]{0:T(128)S(1)} %get-tuple-element.83, f32[12]{0:T(128)S(1)} %get-tuple-element.84, f32[12]{0:T(128)S(1)} %get-tuple-element.85, f32[12]{0:T(128)S(1)} %get-tuple-element.86, f32[12]{0:T(128)S(1)} %get-tuple-element.87, f32[12]{0:T(128)S(1)} %get-tuple-element.88, ...), kind=kLoop, calls=%fused_computation.69 | loop fusion | flops 18874368 | bytes 3933696 | tf_op jit(solution)/shard_map/jit(_where)/select_n | solution.py:61
  96.0 7.6 collective-permute-done.2
  103.6 4.8 collective-permute-done.3
  111.4 7.2 convolution_convert_fusion.1
  120.0 26.4 %attend_forward.2 = (bf16[1,512,768]{2,1,0:T(8,128)(2,1)}, bf16[1,12,512,128]{3,2,1,0:T(8,128)(2,1)}) custom-call(f32[4]{0:T(128)} %add_convert_fusion.flags, bf16[1,512,768]{2,1,0:T(8,128)(2,1)} %get-tuple-element.149.q, bf16[1,4,512,1536]{3,2,1,0:T(8,128)(2,1)} %bitcast.253, bf16[1,4,512,128]{3,2,1,0:T(8,128)(2,1)} %get-tuple-element.151.klanes, ...), custom_call_target="tpu_custom_call" | custom-call | flops 6442450944 | bytes 9437184 | tf_op jit(solution)/shard_map/attend_forward/pallas_call | solution.py:160
  146.4 7.1 convolution_convert_fusion
  153.4 5.5 all-to-all-start.4
  159.0 26.3 %attend_forward.3 = (bf16[1,512,768]{2,1,0:T(8,128)(2,1)}, bf16[1,12,512,128]{3,2,1,0:T(8,128)(2,1)}) custom-call(f32[4]{0:T(128)} %add_convert_fusion.flags, bf16[1,512,768]{2,1,0:T(8,128)(2,1)} %get-tuple-element.150.q, bf16[1,4,512,1536]{3,2,1,0:T(8,128)(2,1)} %bitcast.251, bf16[1,4,512,128]{3,2,1,0:T(8,128)(2,1)} %get-tuple-element.152.klanes, ...), custom_call_target="tpu_custom_call" | custom-call | flops 6442450944 | bytes 9437184 | tf_op jit(solution)/shard_map/attend_forward/pallas_call | solution.py:160
  192.9 5.1 all-to-all-start.3
  202.4 20.9 %all-to-all-done.3 = bf16[8,80,768]{2,1,0:T(8,128)(2,1)} async-done(((bf16[8,80,768]{2,1,0:T(8,128)(2,1)}), bf16[8,80,768]{2,1,0:T(8,128)(2,1)}, u32[]{:S(2)}, u32[]{:S(2)}) %all-to-all-start.3) | async-done | bytes 983072 | tf_op jit(solution)/shard_map/all_to_all | solution.py:520
  223.3 4.5 all-to-all-start
  228.6 7.8 convolution_convert_fusion.6.units
  236.4 16.3 %all-gather.5.cloned.1.call-done.w_in = bf16[2,768,3072]{2,1,0:T(8,128)(2,1)} async-done(((bf16[2,768,768]{2,1,0:T(8,128)(2,1)}), bf16[2,768,3072]{2,1,0:T(8,128)(2,1)}) %all-gather.5.cloned.1.call-update) | async-done | bytes 9437200 | tf_op jit(solution)/shard_map/all_gather | solution.py:493
  252.8 23.0 %run_expert.3 = (bf16[640,3072]{1,0:T(8,128)(2,1)}, bf16[640,3072]{1,0:T(8,128)(2,1)}, bf16[640,768]{1,0:T(8,128)(2,1)}, bf16[640,768]{1,0:T(8,128)(2,1)}, bf16[...) custom-call(s32[1]{0:T(128)} %bitcast.39.own, bf16[640,768]{1,0:T(8,128)(2,1)} %bitcast.41.x, bf16[640,768]{1,0:T(8,128)(2,1)} %bitcast.43.c, ...), custom_call_target="tpu_custom_call" | custom-call | flops 9059696640 | bytes 21233664 | tf_op jit(solution)/shard_map/run_expert/pallas_call | solution.py:385
  275.8 5.1 all-to-all-start.5
  281.0 7.8 convolution_convert_fusion.7.units
  288.8 23.0 %run_expert.2 = (bf16[640,3072]{1,0:T(8,128)(2,1)}, bf16[640,3072]{1,0:T(8,128)(2,1)}, bf16[640,768]{1,0:T(8,128)(2,1)}, bf16[640,768]{1,0:T(8,128)(2,1)}, bf16[...) custom-call(s32[1]{0:T(128)} %bitcast.30.own, bf16[640,768]{1,0:T(8,128)(2,1)} %bitcast.32.x, bf16[640,768]{1,0:T(8,128)(2,1)} %bitcast.35.c, ...), custom_call_target="tpu_custom_call" | custom-call | flops 9059696640 | bytes 21233664 | tf_op jit(solution)/shard_map/run_expert/pallas_call | solution.py:385
  311.8 5.1 all-to-all-start.2
  317.1 4.5 fusion.31
  321.7 20.6 %all-to-all-done.2 = bf16[8,80,768]{2,1,0:T(8,128)(2,1)} async-done(((bf16[8,80,768]{2,1,0:T(8,128)(2,1)}), bf16[8,80,768]{2,1,0:T(8,128)(2,1)}, u32[]{:S(2)}, u32[]{:S(2)}) %all-to-all-start.2) | async-done | bytes 983072 | tf_op jit(solution)/shard_map/all_to_all | solution.py:524
  342.2 6.1 multiply_reduce_fusion
  356.1 35.7 %attend_backward.2 = (bf16[1,512,768]{2,1,0:T(8,128)(2,1)}, bf16[1,4,512,1536]{3,2,1,0:T(8,128)(2,1)}, f32[1,12,32,128]{3,2,1,0:T(8,128)}) custom-call(f32[4]{0:T(128)} %add_convert_fusion.flags, bf16[1,12,512,128]{3,2,1,0:T(8,128)(2,1)} %get-tuple-element.48.qaug, bf16[1,4,512,1536]{3,2,1,0:T(8,128)(2,1)} %bitcast.254, ...), custom_call_target="tpu_custom_call" | custom-call | flops 16106127360 | bytes 15728640 | tf_op jit(solution)/shard_map/attend_backward/pallas_call | solution.py:274
  391.9 35.7 %attend_backward.3 = (bf16[1,512,768]{2,1,0:T(8,128)(2,1)}, bf16[1,4,512,1536]{3,2,1,0:T(8,128)(2,1)}, f32[1,12,32,128]{3,2,1,0:T(8,128)}) custom-call(f32[4]{0:T(128)} %add_convert_fusion.flags, bf16[1,12,512,128]{3,2,1,0:T(8,128)(2,1)} %get-tuple-element.50.qaug, bf16[1,4,512,1536]{3,2,1,0:T(8,128)(2,1)} %bitcast.252, ...), custom_call_target="tpu_custom_call" | custom-call | flops 16106127360 | bytes 15728640 | tf_op jit(solution)/shard_map/attend_backward/pallas_call | solution.py:274
  427.5 16.0 %fusion.12 = f32[768,1536]{1,0:T(8,128)} fusion(bf16[1,4,512,1536]{3,2,1,0:T(8,128)(2,1)} %get-tuple-element.51, bf16[1,4,512,1536]{3,2,1,0:T(8,128)(2,1)} %get-tuple-element.49, bf16[1,4,512,768]{3,2,1,0:T(8,128)(2,1)S(1)} %copy-done.10, bf16[1,4,512,768]{3,2,1,0:T(8,128)(2,1)} %get-tuple-element.129), kind=kOutput, calls=%fused_computation.26 | convolution fusion | flops 9673113600 | bytes 23592960 | tf_op jit(solution)/shard_map/dot_general | solution.py:22
  443.6 6.6 reshape.1236
  455.8 8.6 fusion.9
  464.4 5.8 fusion.10
  470.2 8.3 pad_maximum_fusion.1
  478.6 8.7 fusion.7
  487.3 6.7 fusion.8
  494.0 8.5 pad_maximum_fusion
  508.4 9.5 %fusion.130 = (bf16[2048,768]{1,0:T(8,128)(2,1)S(1)}, f32[2048,768]{1,0:T(8,128)}) fusion(bf16[2048,1536]{1,0:T(8,128)(2,1)} %bitcast.256, bf16[768,1536]{0,1:T(8,128)(2,1)} %bitcast.218), kind=kOutput, calls=%fused_computation.339 | convolution fusion | flops 4833411072 | bytes 18087936 | tf_op jit(solution)/shard_map/dot_general | solution.py:22
  521.8 9.8 %fusion.129 = (bf16[2048,768]{1,0:T(8,128)(2,1)S(1)}, f32[2048,768]{1,0:T(8,128)}) fusion(bf16[2048,1536]{1,0:T(8,128)(2,1)} %bitcast.255, bf16[768,1536]{0,1:T(8,128)(2,1)S(1)} %bitcast.220), kind=kOutput, calls=%fused_computation.338 | convolution fusion | flops 4833411072 | bytes 18087936 | tf_op jit(solution)/shard_map/dot_general | solution.py:22
  551.4 14.2 %collective-permute-done.9 = bf16[512,768]{1,0:T(8,128)(2,1)S(1)} collective-permute-done((bf16[512,768]{1,0:T(8,128)(2,1)S(1)}, bf16[512,768]{1,0:T(8,128)(2,1)S(1)}, u32[]{:S(2)}, u32[]{:S(2)}) %collective-permute-start.9) | collective-permute-done | bytes 786464 | tf_op jit(solution)/shard_map/ppermute | solution.py:432
  571.6 10.3 %collective-permute-done.13 = bf16[512,768]{1,0:T(8,128)(2,1)S(1)} collective-permute-done((bf16[512,768]{1,0:T(8,128)(2,1)S(1)}, bf16[512,768]{1,0:T(8,128)(2,1)S(1)}, u32[]{:S(2)}, u32[]{:S(2)}) %collective-permute-start.13) | collective-permute-done | bytes 786464 | tf_op jit(solution)/shard_map/ppermute | solution.py:432
  581.9 5.1 collective-permute-done.15
  589.8 5.2 all-to-all-start.6
  595.0 5.7 fusion.26
  600.7 45.7 %all-reduce = (f32[768]{0:T(1024)}, f32[32,12]{0,1:T(8,128)}, f32[768]{0:T(1024)}, f32[768,16]{0,1:T(8,128)}) all-reduce(f32[768]{0:T(1024)S(1)} %get-tuple-element.64, f32[32,12]{0,1:T(8,128)S(1)} %fusion.59, f32[768]{0:T(1024)S(1)} %copy-done.44, f32[768,16]{0,1:T(8,128)S(1)} %copy-done.26), channel_id=1, replica_groups=mesh['narrow'=4,'wide'=8] {'narrow','wide'}, use_global_device_ids=true, to_apply=%region_6.7 | all-reduce | flops 14208 | bytes 113664 | tf_op jit(solution)/shard_map/psum | solution.py:599
  646.4 7.5 fusion.25
  653.9 4.5 fusion.30
  658.5 6.5 add_add_fusion
  665.0 15.8 %slice_reduce_fusion = (f32[768,6,128]{2,1,0:T(8,128)S(1)}, f32[768,6,128]{2,1,0:T(8,128)S(1)}) fusion(f32[768,6,2,128]{3,2,1,0:T(2,128)} %get-tuple-element.121), kind=kLoop, calls=%fused_computation.66 | loop fusion | bytes 9437184 | tf_op jit(solution)/shard_map/slice | solution.py:611
  684.6 78.5 %reduce-scatter.5.cloned.1.call-done = bf16[2,768,768]{2,1,0:T(8,128)(2,1)} async-done(((bf16[2,3072,768]{2,1,0:T(8,128)(2,1)}), bf16[2,768,768]{2,1,0:T(8,128)(2,1)}) %reduce-scatter.5.cloned.1.call-update) | async-done | bytes 2359312 | tf_op jit(solution)/shard_map/reduce_scatter | solution.py:558
  767.3 94.1 %reduce-scatter.3.cloned.1.call-done = bf16[2,768,768]{2,1,0:T(8,128)(2,1)} async-done(((bf16[2,768,3072]{2,1,0:T(8,128)(2,1)}), bf16[2,768,768]{2,1,0:T(8,128)(2,1)}) %reduce-scatter.3.cloned.1.call-update) | async-done | bytes 2359312 | tf_op jit(solution)/shard_map/reduce_scatter | solution.py:555
  (299 shorter events, 136.7 us)
Async XLA Ops:
  7.2 79.0 %copy-start = (bf16[768,768]{1,0:T(8,128)(2,1)S(1)}, bf16[768,768]{1,0:T(8,128)(2,1)}, u32[]{:S(2)}) copy-start(bf16[768,768]{1,0:T(8,128)(2,1)} %param.18) | copy-start | bytes 3538948
  7.2 221.4 %all-gather.3.cloned.1.call-start = ((), (), s32[]{:S(2)}) async-start(), calls=%async_computation.10 | async-start | bytes 11796480 | tf_op jit(solution)/shard_map/all_gather | solution.py:494
  12.1 23.6 %copy-start.8 = (bf16[1024,768]{1,0:T(8,128)(2,1)}, bf16[1024,768]{1,0:T(8,128)(2,1)S(1)}, u32[]{:S(2)}) copy-start(bf16[1024,768]{1,0:T(8,128)(2,1)S(1)} %fusion.21) | copy-start | bytes 4718596
  13.4 20.5 %collective-permute-start.5 = (bf16[512,768]{1,0:T(8,128)(2,1)S(1)}, bf16[512,768]{1,0:T(8,128)(2,1)S(1)}, u32[]{:S(2)}, u32[]{:S(2)}) collective-permute-start(bf16[512,768]{1,0:T(8,128)(2,1)S(1)} %get-tuple-element.147), channel_id=1, source_target_pairs={{0,16},{8,24},{16,0},{24,8},{1,17},{9,25},{17,1},{25,9},{2,18},{10... | collective-permute-start | bytes 2359304 | tf_op jit(solution)/shard_map/ppermute | solution.py:432
  16.4 19.4 %collective-permute-start.4 = (bf16[512,768]{1,0:T(8,128)(2,1)S(1)}, bf16[512,768]{1,0:T(8,128)(2,1)S(1)}, u32[]{:S(2)}, u32[]{:S(2)}) collective-permute-start(bf16[512,768]{1,0:T(8,128)(2,1)S(1)} %get-tuple-element.147), channel_id=1, source_target_pairs={{0,8},{8,0},{16,24},{24,16},{1,9},{9,1},{17,25},{25,17},{2,10},{10... | collective-permute-start | bytes 2359304 | tf_op jit(solution)/shard_map/ppermute | solution.py:432
  33.9 10.4 %collective-permute-start.6 = (bf16[256,768]{1,0:T(8,128)(2,1)S(1)}, bf16[256,768]{1,0:T(8,128)(2,1)S(1)}, u32[]{:S(2)}, u32[]{:S(2)}) collective-permute-start(bf16[256,768]{1,0:T(8,128)(2,1)S(1)} %slice.437), channel_id=1, source_target_pairs={{0,8},{8,0},{16,24},{24,16},{1,9},{9,1},{17,25},{25,17},{2,10},{10... | collective-permute-start | bytes 1179656 | tf_op jit(solution)/shard_map/ppermute | solution.py:432
  35.8 9.8 %collective-permute-start.7 = (bf16[256,768]{1,0:T(8,128)(2,1)S(1)}, bf16[256,768]{1,0:T(8,128)(2,1)S(1)}, u32[]{:S(2)}, u32[]{:S(2)}) collective-permute-start(bf16[256,768]{1,0:T(8,128)(2,1)S(1)} %slice.438), channel_id=1, source_target_pairs={{0,16},{8,24},{16,0},{24,8},{1,17},{9,25},{17,1},{25,9},{2,18},{10... | collective-permute-start | bytes 1179656 | tf_op jit(solution)/shard_map/ppermute | solution.py:432
  45.6 7.2 copy-start.45
  48.6 204.2 %all-gather.5.cloned.1.call-start = ((), (), s32[]{:S(2)}) async-start(), calls=%async_computation.11 | async-start | bytes 11796480 | tf_op jit(solution)/shard_map/all_gather | solution.py:493
  48.6 40.4 %collective-permute-start.1 = (bf16[512,768]{1,0:T(8,128)(2,1)}, bf16[512,768]{1,0:T(8,128)(2,1)}, u32[]{:S(2)}, u32[]{:S(2)}) collective-permute-start(bf16[512,768]{1,0:T(8,128)(2,1)} %get-tuple-element.148), channel_id=1, source_target_pairs={{0,16},{8,24},{16,0},{24,8},{1,17},{9,25},{17,1},{25,9},{2,18},{10... | collective-permute-start | bytes 2359304 | tf_op jit(solution)/shard_map/ppermute | solution.py:432
  50.2 41.4 %collective-permute-start = (bf16[512,768]{1,0:T(8,128)(2,1)}, bf16[512,768]{1,0:T(8,128)(2,1)}, u32[]{:S(2)}, u32[]{:S(2)}) collective-permute-start(bf16[512,768]{1,0:T(8,128)(2,1)} %get-tuple-element.148), channel_id=1, source_target_pairs={{0,8},{8,0},{16,24},{24,16},{1,9},{9,1},{17,25},{25,17},{2,10},{10... | collective-permute-start | bytes 2359304 | tf_op jit(solution)/shard_map/ppermute | solution.py:432
  56.2 97.2 %all-to-all-start.1 = ((bf16[8,80,768]{2,1,0:T(8,128)(2,1)}), bf16[8,80,768]{2,1,0:T(8,128)(2,1)}, u32[]{:S(2)}, u32[]{:S(2)}) async-start(bf16[8,80,768]{2,1,0:T(8,128)(2,1)} %bitcast.230), calls=%async_computation.1 | async-start | bytes 1966080 | tf_op jit(solution)/shard_map/all_to_all | solution.py:520
  68.8 42.5 %copy-start.12 = (bf16[768,6,2,128]{0,3,2,1:T(8,128)(2,1)}, bf16[768,6,2,128]{0,3,2,1:T(8,128)(2,1)S(1)}, u32[]{:S(2)}) copy-start(bf16[768,6,2,128]{0,3,2,1:T(8,128)(2,1)S(1)} %copy.407) | copy-start | bytes 7077892
  71.7 22.0 %copy-start.55 = (s32[1024]{0:T(1024)}, s32[1024]{0:T(1024)S(1)}, u32[]{:S(2)}) copy-start(s32[1024]{0:T(1024)S(1)} %and_select_fusion) | copy-start | bytes 12292
  90.0 13.5 %collective-permute-start.2 = (bf16[256,768]{1,0:T(8,128)(2,1)S(1)}, bf16[256,768]{1,0:T(8,128)(2,1)S(1)}, u32[]{:S(2)}, u32[]{:S(2)}) collective-permute-start(bf16[256,768]{1,0:T(8,128)(2,1)S(1)} %slice.398), channel_id=1, source_target_pairs={{0,8},{8,0},{16,24},{24,16},{1,9},{9,1},{17,25},{25,17},{2,10},{10... | collective-permute-start | bytes 1179656 | tf_op jit(solution)/shard_map/ppermute | solution.py:432
  92.6 15.7 %collective-permute-start.3 = (bf16[256,768]{1,0:T(8,128)(2,1)S(1)}, bf16[256,768]{1,0:T(8,128)(2,1)S(1)}, u32[]{:S(2)}, u32[]{:S(2)}) collective-permute-start(bf16[256,768]{1,0:T(8,128)(2,1)S(1)} %slice.399), channel_id=1, source_target_pairs={{0,16},{8,24},{16,0},{24,8},{1,17},{9,25},{17,1},{25,9},{2,18},{10... | collective-permute-start | bytes 1179656 | tf_op jit(solution)/shard_map/ppermute | solution.py:432
  111.4 7.2 copy-start.32
  120.0 26.4 %copy-start.11 = (bf16[4,512,768]{2,1,0:T(8,128)(2,1)S(1)}, bf16[4,512,768]{2,1,0:T(8,128)(2,1)}, u32[]{:S(2)}) copy-start(bf16[4,512,768]{2,1,0:T(8,128)(2,1)} %get-tuple-element.132) | copy-start | bytes 9437188
  120.0 26.4 %copy-start.13 = (bf16[768,6,2,128]{0,3,2,1:T(8,128)(2,1)S(1)}, bf16[768,6,2,128]{0,3,2,1:T(8,128)(2,1)}, u32[]{:S(2)}) copy-start(bf16[768,6,2,128]{0,3,2,1:T(8,128)(2,1)} %copy-done.12) | copy-start | bytes 7077892
  153.4 39.5 %all-to-all-start.4 = ((bf16[8,80,768]{2,1,0:T(8,128)(2,1)}), bf16[8,80,768]{2,1,0:T(8,128)(2,1)}, u32[]{:S(2)}, u32[]{:S(2)}) async-start(bf16[8,80,768]{2,1,0:T(8,128)(2,1)} %bitcast.42), calls=%async_computation.4 | async-start | bytes 1966080 | tf_op jit(solution)/shard_map/all_to_all | solution.py:520
  159.0 26.3 %copy-start.22 = (bf16[1,512,768]{2,1,0:T(8,128)(2,1)S(1)}, bf16[1,512,768]{2,1,0:T(8,128)(2,1)}, u32[]{:S(2)}) copy-start(bf16[1,512,768]{2,1,0:T(8,128)(2,1)} %get-tuple-element.38.att) | copy-start | bytes 2359300
  190.4 7.6 copy-start.37
  192.9 30.4 %all-to-all-start.3 = ((bf16[8,80,768]{2,1,0:T(8,128)(2,1)}), bf16[8,80,768]{2,1,0:T(8,128)(2,1)}, u32[]{:S(2)}, u32[]{:S(2)}) async-start(bf16[8,80,768]{2,1,0:T(8,128)(2,1)} %bitcast.235), calls=%async_computation.3 | async-start | bytes 1966080 | tf_op jit(solution)/shard_map/all_to_all | solution.py:520
  198.0 29.8 %copy-start.41 = (bf16[768,16]{0,1:T(8,128)(2,1)S(1)}, bf16[768,16]{0,1:T(8,128)(2,1)}, u32[]{:S(2)}) copy-start(bf16[768,16]{0,1:T(8,128)(2,1)} %param.24) | copy-start | bytes 73732
  223.3 52.5 %all-to-all-start = ((bf16[8,80,768]{2,1,0:T(8,128)(2,1)}), bf16[8,80,768]{2,1,0:T(8,128)(2,1)}, u32[]{:S(2)}, u32[]{:S(2)}) async-start(bf16[8,80,768]{2,1,0:T(8,128)(2,1)} %bitcast.232), calls=%async_computation | async-start | bytes 1966080 | tf_op jit(solution)/shard_map/all_to_all | solution.py:520
  275.8 36.0 %all-to-all-start.5 = ((bf16[8,80,768]{2,1,0:T(8,128)(2,1)}), bf16[8,80,768]{2,1,0:T(8,128)(2,1)}, u32[]{:S(2)}, u32[]{:S(2)}) async-start(bf16[8,80,768]{2,1,0:T(8,128)(2,1)} %bitcast.233), calls=%async_computation.5 | async-start | bytes 1966080 | tf_op jit(solution)/shard_map/all_to_all | solution.py:524
  311.8 30.4 %all-to-all-start.2 = ((bf16[8,80,768]{2,1,0:T(8,128)(2,1)}), bf16[8,80,768]{2,1,0:T(8,128)(2,1)}, u32[]{:S(2)}, u32[]{:S(2)}) async-start(bf16[8,80,768]{2,1,0:T(8,128)(2,1)} %bitcast.234), calls=%async_computation.2 | async-start | bytes 1966080 | tf_op jit(solution)/shard_map/all_to_all | solution.py:524
  316.9 348.0 %all-reduce.4.cloned.1.call-start = ((), (), s32[]{:S(2)}) async-start(), calls=%async_computation.14 | async-start | bytes 18874368 | tf_op jit(solution)/shard_map/psum | solution.py:599
  391.9 35.7 %copy-start.10 = (bf16[1,4,512,768]{3,2,1,0:T(8,128)(2,1)S(1)}, bf16[1,4,512,768]{3,2,1,0:T(8,128)(2,1)}, u32[]{:S(2)}) copy-start(bf16[1,4,512,768]{3,2,1,0:T(8,128)(2,1)} %get-tuple-element.131) | copy-start | bytes 9437188
  455.8 307.3 %reduce-scatter.5.cloned.1.call-start = ((), (), s32[]{:S(2)}) async-start(), calls=%async_computation.13 | async-start | bytes 11796480 | tf_op jit(solution)/shard_map/reduce_scatter | solution.py:558
  455.8 8.6 copy-start.66
  455.8 8.6 copy-start.67
  478.5 382.9 %reduce-scatter.3.cloned.1.call-start = ((), (), s32[]{:S(2)}) async-start(), calls=%async_computation.12 | async-start | bytes 11796480 | tf_op jit(solution)/shard_map/reduce_scatter | solution.py:555
  478.5 8.7 copy-start.65
  519.0 22.8 %collective-permute-start.10 = (bf16[256,768]{1,0:T(8,128)(2,1)}, bf16[256,768]{1,0:T(8,128)(2,1)}, u32[]{:S(2)}, u32[]{:S(2)}) collective-permute-start(bf16[256,768]{1,0:T(8,128)(2,1)} %get-tuple-element.135), channel_id=1, source_target_pairs={{0,8},{8,0},{16,24},{24,16},{1,9},{9,1},{17,25},{25,17},{2,10},{10... | collective-permute-start | bytes 1179656 | tf_op jit(solution)/shard_map/ppermute | solution.py:432
  520.4 21.3 %collective-permute-start.8 = (bf16[256,768]{1,0:T(8,128)(2,1)}, bf16[256,768]{1,0:T(8,128)(2,1)}, u32[]{:S(2)}, u32[]{:S(2)}) collective-permute-start(bf16[256,768]{1,0:T(8,128)(2,1)} %get-tuple-element.136), channel_id=1, source_target_pairs={{0,16},{8,24},{16,0},{24,8},{1,17},{9,25},{17,1},{25,9},{2,18},{10... | collective-permute-start | bytes 1179656 | tf_op jit(solution)/shard_map/ppermute | solution.py:432
  533.4 13.5 %collective-permute-start.12 = (bf16[256,768]{1,0:T(8,128)(2,1)}, bf16[256,768]{1,0:T(8,128)(2,1)}, u32[]{:S(2)}, u32[]{:S(2)}) collective-permute-start(bf16[256,768]{1,0:T(8,128)(2,1)} %get-tuple-element.140), channel_id=1, source_target_pairs={{0,16},{8,24},{16,0},{24,8},{1,17},{9,25},{17,1},{25,9},{2,18},{10... | collective-permute-start | bytes 1179656 | tf_op jit(solution)/shard_map/ppermute | solution.py:432
  534.9 12.0 %collective-permute-start.14 = (bf16[256,768]{1,0:T(8,128)(2,1)}, bf16[256,768]{1,0:T(8,128)(2,1)}, u32[]{:S(2)}, u32[]{:S(2)}) collective-permute-start(bf16[256,768]{1,0:T(8,128)(2,1)} %get-tuple-element.139), channel_id=1, source_target_pairs={{0,8},{8,0},{16,24},{24,16},{1,9},{9,1},{17,25},{25,17},{2,10},{10... | collective-permute-start | bytes 1179656 | tf_op jit(solution)/shard_map/ppermute | solution.py:432
  535.5 54.3 %all-to-all-start.7 = ((bf16[8,80,768]{2,1,0:T(8,128)(2,1)}), bf16[8,80,768]{2,1,0:T(8,128)(2,1)}, u32[]{:S(2)}, u32[]{:S(2)}) async-start(bf16[8,80,768]{2,1,0:T(8,128)(2,1)} %bitcast.231), calls=%async_computation.7 | async-start | bytes 1966080 | tf_op jit(solution)/shard_map/all_to_all | solution.py:524
  543.6 22.0 %collective-permute-start.9 = (bf16[512,768]{1,0:T(8,128)(2,1)S(1)}, bf16[512,768]{1,0:T(8,128)(2,1)S(1)}, u32[]{:S(2)}, u32[]{:S(2)}) collective-permute-start(bf16[512,768]{1,0:T(8,128)(2,1)S(1)} %pad_maximum_fusion.8), channel_id=1, source_target_pairs={{0,8},{8,0},{16,24},{24,16},{1,9},{9,1},{17,25},{25,17},{2,10},{10... | collective-permute-start | bytes 2359304 | tf_op jit(solution)/shard_map/ppermute | solution.py:432
  545.2 23.6 %collective-permute-start.11 = (bf16[512,768]{1,0:T(8,128)(2,1)S(1)}, bf16[512,768]{1,0:T(8,128)(2,1)S(1)}, u32[]{:S(2)}, u32[]{:S(2)}) collective-permute-start(bf16[512,768]{1,0:T(8,128)(2,1)S(1)} %pad_maximum_fusion.9), channel_id=1, source_target_pairs={{0,16},{8,24},{16,0},{24,8},{1,17},{9,25},{17,1},{25,9},{2,18},{10... | collective-permute-start | bytes 2359304 | tf_op jit(solution)/shard_map/ppermute | solution.py:432
  548.8 33.1 %collective-permute-start.13 = (bf16[512,768]{1,0:T(8,128)(2,1)S(1)}, bf16[512,768]{1,0:T(8,128)(2,1)S(1)}, u32[]{:S(2)}, u32[]{:S(2)}) collective-permute-start(bf16[512,768]{1,0:T(8,128)(2,1)S(1)} %pad_maximum_fusion.10), channel_id=1, source_target_pairs={{0,8},{8,0},{16,24},{24,16},{1,9},{9,1},{17,25},{25,17},{2,10},{10... | collective-permute-start | bytes 2359304 | tf_op jit(solution)/shard_map/ppermute | solution.py:432
  550.5 36.5 %collective-permute-start.15 = (bf16[512,768]{1,0:T(8,128)(2,1)S(1)}, bf16[512,768]{1,0:T(8,128)(2,1)S(1)}, u32[]{:S(2)}, u32[]{:S(2)}) collective-permute-start(bf16[512,768]{1,0:T(8,128)(2,1)S(1)} %pad_maximum_fusion.11), channel_id=1, source_target_pairs={{0,16},{8,24},{16,0},{24,8},{1,17},{9,25},{17,1},{25,9},{2,18},{10... | collective-permute-start | bytes 2359304 | tf_op jit(solution)/shard_map/ppermute | solution.py:432
  571.6 23.3 %copy-start.40 = (f32[1,4,2,128]{3,1,2,0:T(4,128)S(1)}, f32[1,4,2,128]{3,1,2,0:T(4,128)}, u32[]{:S(2)}) copy-start(f32[1,4,2,128]{3,1,2,0:T(4,128)} %copy-done.39) | copy-start | bytes 12292
  571.6 23.3 %copy-start.43 = (f32[768]{0:T(1024)S(1)}, f32[768]{0:T(1024)}, u32[]{:S(2)}) copy-start(f32[768]{0:T(1024)} %param.17) | copy-start | bytes 9220
  589.8 68.7 %all-to-all-start.6 = ((bf16[8,80,768]{2,1,0:T(8,128)(2,1)}), bf16[8,80,768]{2,1,0:T(8,128)(2,1)}, u32[]{:S(2)}, u32[]{:S(2)}) async-start(bf16[8,80,768]{2,1,0:T(8,128)(2,1)} %bitcast.229), calls=%async_computation.6 | async-start | bytes 1966080 | tf_op jit(solution)/shard_map/all_to_all | solution.py:524
  595.0 51.4 %copy-start.35 = (f32[1024]{0:T(1024)S(1)}, f32[1024]{0:T(1024)}, u32[]{:S(2)}) copy-start(f32[1024]{0:T(1024)} %copy-done.34) | copy-start | bytes 12292
  646.4 7.6 copy-start.57
  (50 other events, 164.0 us)
Sparse Core Ops, SparseCore 0:
  48.7 106.0 all-gather.2
  156.7 96.0 all-gather.4
  455.9 208.6 all-reduce.3
  667.9 95.1 reduce-scatter.4
  766.4 94.9 reduce-scatter.2

commit v2 on v1

v2 whole, which is shorter than its diff:
```python
import functools

import jax
import jax.numpy as jnp
import numpy as np
from jax import lax
from jax.experimental import pallas as pl
from jax.experimental.pallas import tpu as pltpu
from jax.sharding import PartitionSpec as P

epsilon = 1e-06
bucket_edges = (1, 2, 3, 4, 5, 6, 7, 8, 12, 16, 23, 32, 46, 64, 91)
LOG2E = 1.4426950408889634
LN2 = 0.6931471805599453
TILE = 128
VMEM_LIMIT = 56 * 1024 * 1024
NT = (((1,), (1,)), ((), ()))
NN = (((1,), (0,)), ((), ()))
TN = (((0,), (0,)), ((), ()))
BRIEF = pl.CostEstimate(flops=1, bytes_accessed=1, transcendentals=0)
LONG = pl.CostEstimate(flops=12_000_000_000, bytes_accessed=1, transcendentals=0)
BF16 = jnp.bfloat16
F32 = jnp.float32


def dotf(a, b, dims=NN):
    return lax.dot_general(a, b, dims, preferred_element_type=F32)


def rms_factor(values):
    return lax.rsqrt(jnp.mean(values * values, axis=-1, keepdims=True) + epsilon)


def rms_pull(values, factor, gain, grad):
    normal = values * factor
    scaled = grad * gain
    mean = jnp.mean(scaled * normal, axis=-1, keepdims=True)
    return (scaled - normal * mean) * factor, grad * normal


def bucket_of(offsets, bucket_count):
    magnitude = jnp.abs(offsets)
    bucket = jnp.zeros_like(offsets)
    for border in bucket_edges:
        bucket = bucket + (magnitude >= border).astype(jnp.int32)
    return bucket + bucket_count // 2 * (offsets > 0).astype(jnp.int32)


def pieces(x):
    hi = x.astype(BF16)
    rest = x - hi.astype(F32)
    mid = rest.astype(BF16)
    low = (rest - mid.astype(F32)).astype(BF16)
    return hi, mid, low


def tiles_kernel(rows, tiles):
    heads = tiles.shape[0]
    for h in range(heads):
        for d in range(3):
            values = jnp.broadcast_to(rows[h : h + 1, d * TILE : d * TILE + 2 * TILE], (TILE, 2 * TILE))
            moved = pltpu.roll(values, 0, 1, stride=1, stride_axis=0)[:, TILE:].T
            tiles[h, d] = moved
            if d == 0:
                tiles[h, 3] = moved - rows[h : h + 1, 4 * TILE : 5 * TILE]
            if d == 2:
                tiles[h, 4] = moved - rows[h : h + 1, 5 * TILE :]


def bias_tiles(bias_table):
    buckets, heads = bias_table.shape
    bucket = bucket_of(jnp.arange(4 * TILE, dtype=jnp.int32) - 2 * TILE, buckets)
    ends = jnp.repeat(jnp.array([buckets // 2 - 1, buckets - 1], jnp.int32), TILE)
    onehot = jnp.concatenate((bucket, ends))[None] == jnp.arange(buckets, dtype=jnp.int32)[:, None]
    rows = lax.dot_general(
        bias_table * LOG2E, onehot.astype(F32), TN, precision=lax.Precision.HIGHEST
    )
    return pl.pallas_call(
        tiles_kernel,
        out_shape=jax.ShapeDtypeStruct((heads, 5, TILE, TILE), F32),
        name="bias_tiles",
    )(rows)


def query_lanes(bias_table, rows):
    buckets, heads = bias_table.shape
    count = rows // TILE
    code = np.zeros((count, 128), np.int32)
    for lane in range(128):
        k = lane % 64
        for a in range(count):
            if 3 <= k < 9:
                code[a, lane] = k - 2
            elif 9 <= k < 9 + 3 * count:
                t = (k - 9) // 3
                code[a, lane] = 1 + k % 3 if t <= a - 2 else 4 + k % 3 if t >= a + 2 else 0
            elif k == 9 + 3 * count:
                code[a, lane] = 7
    values = pieces(bias_table[buckets // 2 - 1] * LOG2E) + pieces(bias_table[buckets - 1] * LOG2E)
    values = values + (jnp.ones((heads,), BF16),)
    code = jnp.asarray(np.repeat(code, TILE, axis=0))[None]
    lanes = jnp.zeros((heads, rows, 128), BF16)
    for i, value in enumerate(values):
        lanes = jnp.where(code == i + 1, value[:, None, None], lanes)
    return lanes


def key_lanes(me, lengths, rows):
    count = rows // TILE
    shape = (lengths.shape[0], 4, rows, 128)
    lane = lax.broadcasted_iota(jnp.int32, shape, 3) % 64
    place = lax.broadcasted_iota(jnp.int32, shape, 2)
    u = lax.broadcasted_iota(jnp.int32, shape, 1)
    block = me ^ u
    one = lane < 3
    one = one | ((lane >= 3) & (lane < 6) & (block < me))
    one = one | ((lane >= 6) & (lane < 9) & (block > me))
    one = one | ((u == 0) & (lane >= 9) & (lane < 9 + 3 * count) & ((lane - 9) // 3 == place // TILE))
    dead = block * rows + place >= lengths[:, None, None, None]
    masked = (lane == 9 + 3 * count) & dead
    return jnp.where(masked, -1e30, one.astype(F32)).astype(BF16)


def neighbour_flags(me):
    one, three = me ^ 1, me ^ 3
    return jnp.stack((one == me + 1, one == me - 1, three == me + 1, three == me - 1)).astype(F32)


def own_lanes(head, rows):
    lane = lax.broadcasted_iota(jnp.int32, (rows, 128), 1)
    return (lane < 64) if head == 0 else (lane >= 64)


def forward_kernel(flags, q, keys, values, klanes, qlanes, tiles, att, qaug, s_ref):
    rows = q.shape[1]
    count = rows // TILE
    one = jnp.ones((), BF16)
    outs = []
    for h in range(2):
        own = own_lanes(h, rows)
        qa = jnp.where(own, q[0], qlanes[h])
        for u in range(4):
            ka = jnp.where(own, keys[0, u], klanes[0, u])
            start = u * rows
            s_ref[h, :, start : start + rows] = dotf(qa, ka, NT)
            if u == 0:
                for a in range(count):
                    for t in range(max(0, a - 1), min(count, a + 2)):
                        spot = (h, slice(a * 128, a * 128 + 128), slice(t * 128, t * 128 + 128))
                        s_ref[spot] = s_ref[spot] + tiles[h, t - a + 1].T
            if u in (1, 3):
                spot = (h, slice(rows - 128, rows), slice(start, start + 128))
                s_ref[spot] = s_ref[spot] + tiles[h, 4].T * flags[u - 1]
                spot = (h, slice(0, 128), slice(start + rows - 128, start + rows))
                s_ref[spot] = s_ref[spot] + tiles[h, 3].T * flags[u]
        top = jnp.max(s_ref[h], axis=1, keepdims=True)
        total = None
        for u in range(4):
            weights = jnp.exp2(s_ref[h, :, u * rows : (u + 1) * rows] - top).astype(BF16)
            part = dotf(weights, jnp.where(own, values[0, u], one))
            total = part if total is None else total + part
        turned = pltpu.roll(total, 64, 1)
        outs.append(total / turned)
        hi, mid, low = pieces(top + jnp.log2(jnp.where(own, turned, total)))
        lane = lax.broadcasted_iota(jnp.int32, (rows, 128), 1) - (64 if h == 0 else 0)
        qaug[0, h] = jnp.where(
            lane == 0, -hi, jnp.where(lane == 1, -mid, jnp.where(lane == 2, -low, qa))
        )
    att[0] = jnp.where(own_lanes(0, rows), outs[0], outs[1]).astype(BF16)


def attend_forward(seq, cost, flags, q, keys, values, klanes, qlanes, tiles):
    rows, width = q.shape[1:]
    pairs = width // 128
    return pl.pallas_call(
        forward_kernel,
        grid=(pairs,),
        in_specs=[
            pl.BlockSpec(memory_space=pltpu.SMEM),
            pl.BlockSpec((1, rows, 128), lambda p: (seq, 0, p)),
            pl.BlockSpec((1, 4, rows, 128), lambda p: (0, 0, 0, p)),
            pl.BlockSpec((1, 4, rows, 128), lambda p: (0, 0, 0, p)),
            pl.BlockSpec((1, 4, rows, 128), lambda p: (seq, 0, 0, 0)),
            pl.BlockSpec((2, rows, 128), lambda p: (p, 0, 0)),
            pl.BlockSpec((2, 5, TILE, TILE), lambda p: (p, 0, 0, 0)),
        ],
        out_specs=[
            pl.BlockSpec((1, rows, 128), lambda p: (0, 0, p)),
            pl.BlockSpec((1, 2, rows, 128), lambda p: (0, p, 0, 0)),
        ],
        out_shape=[
            jax.ShapeDtypeStruct((1, rows, width), BF16),
            jax.ShapeDtypeStruct((1, 2 * pairs, rows, 128), BF16),
        ],
        scratch_shapes=[pltpu.VMEM((2, rows, 4 * rows), F32)],
        compiler_params=pltpu.CompilerParams(
            dimension_semantics=("arbitrary",), vmem_limit_bytes=VMEM_LIMIT
        ),
        cost_estimate=cost,
        name="attend_forward",
    )(flags, q, keys, values, klanes, qlanes, tiles)


def backward_kernel(flags, qaug, keys, values, att, do, klanes, tiles, dq, dkeys, dvalues, table):
    rows = do.shape[1]
    count = rows // TILE
    own0 = own_lanes(0, rows)
    prod = do[0].astype(F32) * att[0].astype(F32)
    one, zero = jnp.ones((), BF16), jnp.zeros((), BF16)
    turned = []
    for h in range(2):
        own = own_lanes(h, rows)
        qa = qaug[0, h]
        delta = jnp.sum(jnp.where(own, prod, 0.0), axis=1, keepdims=True)
        hi, mid, _ = pieces(jnp.broadcast_to(delta, (rows, 128)))
        lane = lax.broadcasted_iota(jnp.int32, (rows, 128), 1) - (64 if h == 0 else 0)
        doa = jnp.where(own, do[0], jnp.where(lane == 0, -hi, jnp.where(lane == 1, -mid, zero)))
        near = {}
        corner = {-1: None, 1: None}
        dqt = None
        for u in range(4):
            ka = jnp.where(own, keys[0, u], klanes[0, u])
            va = jnp.where(own, values[0, u], one)
            st = dotf(ka, qa, NT)
            if u == 0:
                strips = []
                for t in range(count):
                    row = []
                    for a in range(count):
                        x = st[t * 128 : t * 128 + 128, a * 128 : a * 128 + 128]
                        row.append(x + tiles[h, t - a + 1] if abs(t - a) <= 1 else x)
                    strips.append(jnp.concatenate(row, axis=1))
                st = jnp.concatenate(strips, axis=0)
            if u in (1, 3):
                after, before = flags[u - 1], flags[u]
                first = jnp.concatenate(
                    (st[:128, : rows - 128], st[:128, rows - 128 :] + tiles[h, 4] * after), axis=1
                )
                last = jnp.concatenate(
                    (st[rows - 128 :, :128] + tiles[h, 3] * before, st[rows - 128 :, 128:]), axis=1
                )
                st = jnp.concatenate((first, st[128 : rows - 128], last), axis=0)
            probs = jnp.exp2(st)
            ds = probs * dotf(va, doa, NT)
            probs_low, ds_low = probs.astype(BF16), ds.astype(BF16)
            if u == 0:
                for d in (-1, 0, 1):
                    for a in range(max(0, -d), min(count, count - d)):
                        t = a + d
                        x = ds[t * 128 : t * 128 + 128, a * 128 : a * 128 + 128]
                        near[d] = near[d] + x if d in near else x
            if u in (1, 3):
                for d, x in ((1, ds[:128, rows - 128 :] * after), (-1, ds[rows - 128 :, :128] * before)):
                    corner[d] = x if corner[d] is None else corner[d] + x
            dv = dotf(probs_low, doa).astype(BF16)
            dk = (dotf(ds_low, qa) * LN2).astype(BF16)
            if h == 0:
                dkeys[0, u], dvalues[0, u] = dk, dv
            else:
                dkeys[0, u] = jnp.where(own0, dkeys[0, u], dk)
                dvalues[0, u] = jnp.where(own0, dvalues[0, u], dv)
            part = dotf(ka.T, ds_low)
            dqt = part if dqt is None else dqt + part
        turned.append(dqt.T)
        group = lax.broadcasted_iota(jnp.int32, (TILE, TILE), 0) // 8 * 8
        upper = lax.broadcasted_iota(jnp.int32, (TILE, TILE), 1) >= group
        before, after = near[-1] + corner[-1], near[1] + corner[1]
        inner = (jnp.where(upper, near[0], before), jnp.where(upper, after, near[0]))
        for i, x in enumerate(inner):
            lined = x[:8]
            for g in range(1, TILE // 8):
                lined = lined + pltpu.roll(x[8 * g : 8 * g + 8], TILE - 8 * g, 1)
            table[0, h, 8 * i : 8 * i + 8, :] = lined
        outer = (jnp.where(upper, before, 0.0), jnp.where(upper, 0.0, after), corner[-1], corner[1])
        for i, x in enumerate(outer):
            table[0, h, 16 + i : 17 + i, :] = jnp.sum(x, axis=0, keepdims=True)
    dq[0] = (jnp.where(own0, turned[0], turned[1]) * 0.125).astype(BF16)
    for h in range(2):
        for a in range(count):
            rest = jnp.sum(turned[h][a * 128 : a * 128 + 128], axis=0, keepdims=True)
            table[0, h, 20 + a : 21 + a, :] = rest


def attend_backward(seq, flags, qaug, keys, values, att, do, klanes, tiles):
    rows, width = do.shape[1:]
    pairs = width // 128
    return pl.pallas_call(
        backward_kernel,
        grid=(pairs,),
        in_specs=[
            pl.BlockSpec(memory_space=pltpu.SMEM),
            pl.BlockSpec((1, 2, rows, 128), lambda p: (0, p, 0, 0)),
            pl.BlockSpec((1, 4, rows, 128), lambda p: (0, 0, 0, p)),
            pl.BlockSpec((1, 4, rows, 128), lambda p: (0, 0, 0, p)),
            pl.BlockSpec((1, rows, 128), lambda p: (0, 0, p)),
            pl.BlockSpec((1, rows, 128), lambda p: (seq, 0, p)),
            pl.BlockSpec((1, 4, rows, 128), lambda p: (seq, 0, 0, 0)),
            pl.BlockSpec((2, 5, TILE, TILE), lambda p: (p, 0, 0, 0)),
        ],
        out_specs=[
            pl.BlockSpec((1, rows, 128), lambda p: (0, 0, p)),
            pl.BlockSpec((1, 4, rows, 128), lambda p: (0, 0, 0, p)),
            pl.BlockSpec((1, 4, rows, 128), lambda p: (0, 0, 0, p)),
            pl.BlockSpec((1, 2, 32, 128), lambda p: (0, p, 0, 0)),
        ],
        out_shape=[
            jax.ShapeDtypeStruct((1, rows, width), BF16),
            jax.ShapeDtypeStruct((1, 4, rows, width), BF16),
            jax.ShapeDtypeStruct((1, 4, rows, width), BF16),
            jax.ShapeDtypeStruct((1, 2 * pairs, 32, 128), F32),
        ],
        compiler_params=pltpu.CompilerParams(
            dimension_semantics=("arbitrary",), vmem_limit_bytes=VMEM_LIMIT
        ),
        cost_estimate=BRIEF,
        name="attend_backward",
    )(flags, qaug, keys, values, att, do, klanes, tiles)


def table_grad(table, rows, bucket_count):
    count = rows // TILE
    heads = table.shape[0]
    row = jnp.arange(16, dtype=jnp.int32)[:, None]
    lane = jnp.arange(TILE, dtype=jnp.int32)[None, :]
    bucket = bucket_of(row // 8 * TILE + row % 8 - lane, bucket_count)
    ids = jnp.arange(bucket_count, dtype=jnp.int32)
    onehot = (bucket[None] == ids[:, None, None]).astype(F32)
    near = jnp.einsum("hil,bil->bh", table[:, :16], onehot, precision=lax.Precision.HIGHEST)
    halves = table[:, 20 : 20 + count].reshape(heads // 2, 2, count, 2, 64)
    rest = jnp.stack((halves[:, 0, :, 1], halves[:, 1, :, 0]), axis=1).reshape(heads, count, 64)
    outer = jnp.sum(table[:, 16:20], axis=2)
    left = jnp.sum(rest[:, :, 3], axis=1) + outer[:, 0] - outer[:, 2]
    right = jnp.sum(rest[:, :, 6], axis=1) + outer[:, 1] - outer[:, 3]
    for a in range(count):
        for t in range(count):
            if t <= a - 2:
                left = left + rest[:, a, 9 + 3 * t]
            if t >= a + 2:
                right = right + rest[:, a, 9 + 3 * t]
    far = jnp.where((ids == bucket_count // 2 - 1)[:, None], left[None, :], 0.0)
    return near + far + jnp.where((ids == bucket_count - 1)[:, None], right[None, :], 0.0)


def expert_kernel(experts, fresh, own, x, c, in0, in1, in2, in3, out0, out1, out2, out3, router, *refs):
    (hidden, grad_pre, low_c, back, grad_x, grad_logits) = refs[0 if fresh else 3 :][:6]
    gate_ref, probs_ref, out_acc, x_acc, w_in, w_out, sems = refs[-7:]
    step = pl.program_id(0)
    ins, outs = (in0, in1, in2, in3), (out0, out1, out2, out3)
    rows = x.shape[0]

    def fetch(u):
        return (
            pltpu.make_async_copy(ins[u], w_in.at[u], sems.at[0, u]),
            pltpu.make_async_copy(outs[u], w_out.at[u], sems.at[1, u]),
        )

    for u in range(4):

        @pl.when(step == max(u - 1, 0))
        def _():
            for copy in fetch(u):
                copy.start()

    @pl.when(step == 0)
    def _():
        ids = lax.broadcasted_iota(jnp.int32, probs_ref.shape, 1)
        logits = jnp.where(ids < experts, dotf(x[...], router[...]), -1e30)
        weights = jnp.exp(logits - jnp.max(logits, axis=1, keepdims=True))
        probs = weights / jnp.sum(weights, axis=1, keepdims=True)
        probs_ref[...] = probs
        gate = jnp.sum(jnp.where(ids == own[0], probs, 0.0), axis=1, keepdims=True)
        gate_ref[...] = jnp.broadcast_to(gate, gate_ref.shape)
        low_c[...] = (c[...].astype(F32) * gate).astype(BF16)
        out_acc[...] = jnp.zeros_like(out_acc)
        x_acc[...] = jnp.zeros_like(x_acc)

    for u in range(4):

        @pl.when(step == u)
        def _():
            for copy in fetch(u):
                copy.wait()

    first, second = w_in[step], w_out[step]
    pre = dotf(x[...], first)
    units = dotf(low_c[...], second, NT)
    below = 0.5 + 0.5 * lax.erf(pre * 0.7071067811865476)
    hid = (pre * below).astype(BF16)
    slope = below + pre * (jnp.exp(pre * pre * -0.5) * 0.3989422804014327)
    low = (slope * units).astype(BF16)
    hidden[0] = hid
    grad_pre[0] = low
    out_acc[...] += dotf(hid, second)
    x_acc[...] += dotf(low, first, NT)

    @pl.when(step == 3)
    def _():
        result = out_acc[...]
        gate = gate_ref[:, :1]
        probs = probs_ref[...]
        grad_gate = jnp.sum(c[...].astype(F32) * result.astype(BF16).astype(F32), axis=1, keepdims=True)
        ids = lax.broadcasted_iota(jnp.int32, probs.shape, 1)
        mine = jnp.where(ids == own[0], 1.0, 0.0)
        logits = (grad_gate * probs * (mine - gate)).astype(BF16)
        grad_logits[...] = logits
        back[...] = (result * gate).astype(BF16)
        grad_x[...] = (x_acc[...] + dotf(logits, router[...], NT)).astype(BF16)


def run_expert(half, experts, own, x, c, ins, outs, router, kept=()):
    rows, width = x.shape
    lanes = router.shape[1]
    whole = lambda u: (0, 0)
    anywhere = pl.BlockSpec(memory_space=pl.ANY)
    blocks = pl.BlockSpec((1, rows, width), lambda u: (u, half, 0))
    both = jax.ShapeDtypeStruct((4, 2 * rows, width), BF16)
    one = jax.ShapeDtypeStruct((rows, width), BF16)
    return pl.pallas_call(
        functools.partial(expert_kernel, experts, not kept),
        grid=(4,),
        in_specs=[
            pl.BlockSpec(memory_space=pltpu.SMEM),
            pl.BlockSpec((rows, width), whole),
            pl.BlockSpec((rows, width), whole),
        ]
        + [anywhere] * 8
        + [pl.BlockSpec((width, lanes), whole)]
        + [anywhere] * len(kept),
        out_specs=[blocks, blocks, pl.BlockSpec((rows, width), lambda u: (half, 0))]
        + [pl.BlockSpec((rows, width), whole)] * 2
        + [pl.BlockSpec((rows, lanes), whole)],
        out_shape=[both, both, jax.ShapeDtypeStruct((2 * rows, width), BF16), one, one]
        + [jax.ShapeDtypeStruct((rows, lanes), BF16)],
        scratch_shapes=[
            pltpu.VMEM((rows, 128), F32),
            pltpu.VMEM((rows, lanes), F32),
            pltpu.VMEM((rows, width), F32),
            pltpu.VMEM((rows, width), F32),
            pltpu.VMEM((4,) + ins[0].shape, BF16),
            pltpu.VMEM((4,) + outs[0].shape, BF16),
            pltpu.SemaphoreType.DMA((2, 4)),
        ],
        input_output_aliases={12 + i: i for i in range(len(kept))},
        compiler_params=pltpu.CompilerParams(
            dimension_semantics=("arbitrary",), vmem_limit_bytes=VMEM_LIMIT
        ),
        cost_estimate=BRIEF,
        name="run_expert",
    )(own, x, c, *ins, *outs, router, *kept)


def swap(x, bit):
    return lax.ppermute(x, "narrow", [(i, i ^ bit) for i in range(4)])


def swap_wide(x, bit):
    return lax.ppermute(x, "wide", [(i, i ^ bit) for i in range(lax.axis_size("wide"))])


def after(x, *others):
    return lax.optimization_barrier((x,) + others)[0]


def pick(x, index):
    return lax.dynamic_index_in_dim(x, index, 0, keepdims=False)


def scatter_blocks(blocks):
    half = blocks[0].shape[0] // 2
    from_one = swap(blocks[3][:half], 1).astype(F32)
    from_two = swap(blocks[3][half:], 2).astype(F32)
    one = jnp.concatenate(
        (blocks[1][:half], (blocks[1][half:].astype(F32) + from_two).astype(BF16)), axis=0
    )
    two = jnp.concatenate(
        ((blocks[2][:half].astype(F32) + from_one).astype(BF16), blocks[2][half:]), axis=0
    )
    return blocks[0].astype(F32) + swap(one, 1).astype(F32) + swap(two, 2).astype(F32)


def sum_everywhere(x):
    wide = lax.axis_index("wide")
    narrow = lax.axis_index("narrow")
    layers = lax.axis_size("wide") // 2
    rows = x.shape[0]
    x = jnp.pad(x.astype(BF16), ((0, -rows % (8 * layers)), (0, 0)))

    def layer_swap(a, k):
        return swap_wide(a, 2 * k)

    levels = ((2, wide % 2, swap_wide), (4, narrow, swap), (layers, wide // 2, layer_swap))
    for count, place, send in levels:
        x = x.reshape(count, x.shape[0] // count, -1)
        total = pick(x, place).astype(F32)
        for k in range(1, count):
            total = total + send(pick(x, place ^ k), k).astype(F32)
        x = total.astype(BF16)
    for count, place, send in reversed(levels):
        parts = jnp.stack([x] + [send(x, k) for k in range(1, count)])
        x = jnp.concatenate([pick(parts, place ^ i) for i in range(count)], axis=0)
    return x[:rows]


def on_device(
    hidden_in,
    lengths,
    routes,
    norm_gain_attn,
    query_weight,
    key_weight,
    value_weight,
    out_weight,
    bias_table,
    norm_gain_ffn,
    router_weight,
    expert_in,
    expert_out,
    cotangent,
):
    wide_count = lax.axis_size("wide")
    seq_count, rows, width = hidden_in.shape
    bucket_count, head_count = bias_table.shape
    pairs = width // 128
    tokens = seq_count * rows
    local_experts = expert_in.shape[0]
    expert_count = local_experts * wide_count
    capacity = 5 * tokens // (4 * expert_count)
    slots = wide_count * capacity
    me = lax.axis_index("narrow")
    near = me // 2
    far = 1 - near
    own = jnp.reshape(lax.axis_index("wide") * local_experts + near, (1,))

    source = hidden_in.astype(F32).reshape(tokens, width)
    factor_attn = rms_factor(source)
    normed = (source * factor_attn * norm_gain_attn).astype(BF16)
    normed_seqs = normed.reshape(seq_count, rows, width)
    queries = (dotf(normed, query_weight) * (LOG2E / 8)).astype(BF16).reshape(seq_count, rows, width)
    flags = neighbour_flags(me)
    klanes = key_lanes(me, lengths, rows)
    qlanes = query_lanes(bias_table, rows)
    tiles = bias_tiles(bias_table)
    router = jnp.pad(router_weight, ((0, 0), (0, -expert_count % 128)))
    shards = [(pick(w, near), pick(w, far)) for w in (expert_in, expert_out)]

    blocks = []
    for s in range(seq_count):
        mine = after(normed_seqs[s], blocks[-1]) if blocks else normed_seqs[s]
        others = [swap(mine, u) for u in range(1, 4)]
        if s == 0:
            first = (others, queries, klanes, qlanes, tiles, router, shards)
            first = lax.optimization_barrier(first)
            others, queries, klanes, qlanes, tiles, router, shards = first
        blocks.append(jnp.stack([mine] + others))

    route = routes.reshape(tokens)
    position = me * rows + jnp.arange(rows, dtype=jnp.int32)
    live = (position[None, :] < lengths[:, None]).reshape(tokens)
    expert_ids = jnp.arange(expert_count, dtype=jnp.int32)
    chosen = ((route[:, None] == expert_ids[None, :]) & live[:, None]).astype(F32)
    token_ids = jnp.arange(tokens, dtype=jnp.int32)
    earlier = (token_ids[:, None] > token_ids[None, :]).astype(BF16)
    place = jnp.sum(dotf(earlier, chosen.astype(BF16)) * chosen, axis=-1).astype(jnp.int32)
    kept = live & (place < capacity)
    slot = route // local_experts * capacity + place
    slot_ids = jnp.arange(slots, dtype=jnp.int32)

    def slot_map(expert):
        due = jnp.where(kept & (route % local_experts == expert), slot, -1)
        return (slot_ids[:, None] == due[None, :]).astype(BF16)

    map_far, map_near = slot_map(far), slot_map(near)

    def exchange(values):
        sent = values.reshape(wide_count, -1, width)
        return lax.all_to_all(sent, "wide", 0, 0, tiled=True)

    cot = cotangent.reshape(tokens, width)
    cot_far = dotf(map_far, cot).astype(BF16).reshape(wide_count, capacity, width)
    cot_near = dotf(map_near, cot).astype(BF16).reshape(wide_count, capacity, width)
    got = exchange(jnp.concatenate((cot_far, cot_near), axis=1).reshape(2 * slots, width))
    cot_far = swap(got[:, :capacity].reshape(slots, width), 2)
    cot_near = got[:, capacity:].reshape(slots, width)

    kvs, atts, qaugs = [], [], []
    for s in range(seq_count):
        rows_all = blocks[s].reshape(4 * rows, width)
        kvs.append(
            [
                dotf(rows_all, w).astype(BF16).reshape(1, 4, rows, width)
                for w in (key_weight, value_weight)
            ]
        )
        cost = LONG if s == 0 else BRIEF
        att, qaug = attend_forward(s, cost, flags, queries, *kvs[s], klanes, qlanes, tiles)
        atts.append(att)
        qaugs.append(qaug)
        if s == 0:
            shards, _ = lax.optimization_barrier((shards, att))
            ins, outs = ([zero, swap(zero, 1), swap(other, 2)] for zero, other in shards)
    attended = jnp.concatenate(atts, axis=0).reshape(tokens, width)
    attended, ins, outs = lax.optimization_barrier((attended, ins, outs))
    residual = source + dotf(attended, out_weight)
    factor_ffn = rms_factor(residual)
    ffn_input = (residual * factor_ffn * norm_gain_ffn).astype(BF16)

    sent_far = dotf(map_far, ffn_input).astype(BF16)
    sent_near = dotf(map_near, after(ffn_input, sent_far, cot_far)).astype(BF16)
    ins.append(swap(after(ins[2], sent_near), 1))
    outs.append(swap(after(outs[2], ins[3]), 1))
    x_far = swap(exchange(sent_far).reshape(slots, width), 2)
    x_near = exchange(sent_near).reshape(slots, width)
    *shared, back_far, grad_x_far, logits_far = run_expert(
        0, expert_count, own, x_far, cot_far, ins, outs, router
    )
    grad_x_far = swap(grad_x_far, 2)
    hidden, grad_pre, low_c, back_near, grad_x_near, logits_near = run_expert(
        1, expert_count, own, x_near, cot_near, ins, outs, router, tuple(shared)
    )
    sent = jnp.concatenate(
        [x.reshape(wide_count, capacity, width) for x in (grad_x_far, grad_x_near)], axis=1
    )
    got = exchange(sent)
    grad_x_far, grad_x_near = (
        x.reshape(slots, width) for x in (got[:, :capacity], got[:, capacity:])
    )

    x_far, x_near, low_c, logits_far, logits_near, _ = lax.optimization_barrier(
        (x_far, x_near, low_c, logits_far, logits_near, sent)
    )
    xs = jnp.concatenate((x_far, x_near), axis=0)
    grad_experts = [None] * 4
    for u in (3, 1, 2, 0):
        both = (dotf(xs, grad_pre[u], TN), dotf(hidden[u], low_c, TN))
        both = jnp.concatenate([x.astype(BF16) for x in both], axis=0)
        grad_experts[u] = swap(both, u) if u else both
    back_far = swap(after(back_far, sent), 2)

    grad_router = dotf(x_far, logits_far, TN) + dotf(x_near, logits_near, TN)

    grad_ffn_input = dotf(map_near, grad_x_near, TN) + dotf(map_far, grad_x_far, TN)
    grad_norm, gain_ffn = rms_pull(residual, factor_ffn, norm_gain_ffn, grad_ffn_input)
    gain_ffn = jnp.sum(gain_ffn, axis=0)
    grad_residual = cot.astype(F32) + grad_norm
    grad_branch = grad_residual.astype(BF16)
    grad_out_weight = dotf(attended, grad_branch, TN)
    grad_attended = dotf(grad_branch, out_weight, NT).astype(BF16).reshape(seq_count, rows, width)
    back = jnp.concatenate(
        [x.reshape(wide_count, capacity, width) for x in (back_far, back_near)], axis=1
    )
    grad_attended, back = lax.optimization_barrier((grad_attended, back))
    back = exchange(back)
    dqs, dks, dvs = [], [], []
    table = 0.0
    for s in range(seq_count):
        dq, dk, dv, table_one = attend_backward(
            s, flags, qaugs[s], *kvs[s], atts[s], after(grad_attended, *dqs), klanes, tiles
        )
        dqs.append(dq.reshape(rows, width))
        dks.append(dk.reshape(4 * rows, width))
        dvs.append(dv.reshape(4 * rows, width))
        table = table + table_one[0]
    dqs, dks, dvs, grad_experts, back = lax.optimization_barrier(
        (dqs, dks, dvs, grad_experts, back)
    )
    summands = [
        sum(dotf(x.reshape(-1, width), g, TN) for x, g in zip(xs, grads))
        for xs, grads in ((normed_seqs, dqs), (blocks, dks), (blocks, dvs))
    ]
    table = table_grad(table, rows, bucket_count)
    rest = jnp.concatenate(
        (
            jnp.pad(table, ((0, 0), (0, width - head_count))),
            grad_router.T[:expert_count],
            gain_ffn[None],
            jnp.zeros((-(bucket_count + expert_count + 1) % 64, width), F32),
        ),
        axis=0,
    )
    summands = [x.astype(BF16) for x in summands + [grad_out_weight, rest]]
    summands, dqs, dks, dvs = lax.optimization_barrier((summands, dqs, dks, dvs))
    sums = sum_everywhere(jnp.concatenate(summands, axis=0)).astype(F32)
    block_out = residual + dotf(map_far, back[:, :capacity].reshape(slots, width), TN)
    block_out = block_out + dotf(map_near, back[:, capacity:].reshape(slots, width), TN)
    zero, one, two, three = (x.astype(F32).reshape(2, 1, width, -1) for x in grad_experts)
    zero, other = zero + one, two + three
    grad_in, grad_out = jnp.where(
        near == 0, jnp.concatenate((zero, other), axis=1), jnp.concatenate((other, zero), axis=1)
    )

    parts = []
    for s in range(seq_count):
        part = dotf(dks[s], key_weight, NT) + dotf(dvs[s], value_weight, NT)
        part = part.astype(BF16).reshape(4, rows, width)
        own_part = dotf(dqs[s], query_weight, NT)
        parts.append(scatter_blocks([part[u] for u in range(4)]) + own_part)
    grad_normed = jnp.concatenate(parts, axis=0)
    grad_hidden = grad_residual + rms_pull(source, factor_attn, norm_gain_attn, grad_normed)[0]

    sum_q, sum_k, sum_v, sum_out = (sums[i * width : (i + 1) * width] for i in range(4))
    sum_rest = sums[4 * width :]
    sum_router = sum_rest[bucket_count : bucket_count + expert_count]
    gain_attn = sum(
        jnp.sum(grad * weight.astype(F32), axis=1)
        for grad, weight in ((sum_q, query_weight), (sum_k, key_weight), (sum_v, value_weight))
    )
    out_shape = (seq_count, rows, width)
    return (
        block_out.reshape(out_shape),
        grad_hidden.reshape(out_shape),
        gain_attn / norm_gain_attn,
        sum_q,
        sum_k,
        sum_v,
        sum_out,
        sum_rest[:bucket_count, :head_count],
        sum_rest[bucket_count + expert_count],
        sum_router.T,
        grad_in,
        grad_out,
    )


def solution(mesh):
    placed = (
        P("wide", "narrow", None),
        P("wide"),
        P("wide", "narrow", None),
        P(),
        P(),
        P(),
        P(),
        P(),
        P(),
        P(),
        P(),
        P("wide", None, "narrow"),
        P("wide", "narrow", None),
        P("wide", "narrow", None),
    )
    return jax.shard_map(
        on_device,
        mesh=mesh,
        in_specs=placed,
        out_specs=(
            P("wide", "narrow", None),
            P("wide", "narrow", None),
            P(),
            P(),
            P(),
            P(),
            P(),
            P(),
            P(),
            P(),
            P("wide", None, "narrow"),
            P("wide", "narrow", None),
        ),
        check_vma=False,
    )
```

time: 883 us -> 625 us (0.71)
  waiting for transfers between devices: 301 us -> 171 us
  blocking collectives: 45.7 us -> 0 us
  matrix products: 148 us -> 104 us
  local copies, waits for them, and re-layouts: 58.6 us -> 40.4 us
  between operations: 15 us -> 2.38 us
  other arithmetic: 77.2 us -> 66.2 us
    reduce_scatter x2 -> x0, waiting for transfers between devices: 173 us -> none  [the longest x1 94.1 us: on_device(): lax.psum_scatter(jnp.stack(grad_in), 'narrow', scatter_dimension=2, tiled...]
    ppermute x16 -> x33, waiting for transfers between devices: 70.4 us -> 130 us  [swap(): return lax.ppermute(x, 'narrow', [(i, i ^ bit) for i in range(4)])]
    psum x1 -> x0, blocking collectives: 45.7 us -> none  [on_device(): lax.psum((grad_q, grad_kv, grad_out_weight, grad_router, grad_table, gain...]
    dot_general x28 -> x39, matrix products: 148 us -> 103 us  [dotf(): return lax.dot_general(a, b, dims, preferred_element_type=F32)]
    another operation x11 -> x6, other arithmetic: 28.1 us -> 4.75 us  [the longest x2 4.23 us: on_device(): blocks.append(jnp.stack([mine] + others))]
    all_to_all x8 -> x5, waiting for transfers between devices: 41.5 us -> 19.2 us  [exchange(): return lax.all_to_all(sent, 'wide', 0, 0, tiled=True)]
    ppermute x0 -> x8, waiting for transfers between devices: none -> 21 us  [swap_wide(): lax.ppermute(x, 'wide', [(i, i ^ bit) for i in range(lax.axis_size('wide'...]
    all_gather x2 -> x0, waiting for transfers between devices: 16.3 us -> none  [the longest x1 16.3 us: on_device(): whole_in = lax.all_gather(expert_in, 'narrow', axis=2, tiled=True)]
  transfers between devices with their start and end apart: 29 -> 46, of which waited for: 15 -> 17; matrix products, arithmetic and copies ran while one was open for 25% -> 24% of each run, Pallas kernels for 11% -> 27%
where the time goes in v2:
time: 625 us; the launch traced here: 620 us
  waiting for transfers between devices  171 us (27%)
  Pallas kernels  168 us (27%)
  matrix products  104 us (17%)
  starting transfers between devices  68.7 us (11%)
  other arithmetic  66.2 us (11%)
  local copies, waits for them, and re-layouts  40.4 us (6%)
    ppermute x33, waiting for transfers between devices, swap(): return lax.ppermute(x, 'narrow', [(i, i ^ bit) for i in range(4)])  130 us
    dot_general x39, matrix products, dotf(): return lax.dot_general(a, b, dims, preferred_element_type=F32)  103 us
    pallas_call x2, Pallas kernels, attend_backward(): pl.pallas_call(backward_kernel, grid=(pairs,), in_specs=[pl.BlockSpec(mem...  71 us
    pallas_call x2, Pallas kernels, attend_forward(): pl.pallas_call(forward_kernel, grid=(pairs,), in_specs=[pl.BlockSpec(memo...  52.4 us
    pallas_call x2, Pallas kernels, run_expert(): pl.pallas_call(functools.partial(expert_kernel, experts, not kept), grid=...  39.4 us
    ppermute x33, starting transfers between devices, swap(): return lax.ppermute(x, 'narrow', [(i, i ^ bit) for i in range(4)])  35.6 us
    all_to_all x5, starting transfers between devices, exchange(): return lax.all_to_all(sent, 'wide', 0, 0, tiled=True)  24.1 us
    ppermute x8, waiting for transfers between devices, swap_wide(): lax.ppermute(x, 'wide', [(i, i ^ bit) for i in range(lax.axis_size('wide'...  21 us
  transfers between devices with their start and end apart: 46, of which 17 were waited for; matrix products, arithmetic and copies ran while one was open for 24% of the time, Pallas kernels for 27%

profile of v2, /device:TPU:0, one launch (start us, length us, event | category | flops | bytes accessed | tf_op | source)
XLA Modules:
  0.0 620.1 jit_solution(3089589545639865079)
XLA Ops:
  17.4 5.6 all-to-all-start.1
  26.9 4.3 multiply_convert_fusion.1
  34.2 4.7 dynamic-slice_bitcast_fusion.1
  42.3 4.7 bias_tiles.1.tiles
  58.2 3.9 convolution_convert_fusion.3
  62.2 4.0 convolution_convert_fusion.2
  66.2 26.3 %attend_forward.2 = (bf16[1,512,768]{2,1,0:T(8,128)(2,1)}, bf16[1,12,512,128]{3,2,1,0:T(8,128)(2,1)}) custom-call(f32[4]{0:T(128)} %add_convert_fusion.9.flags, bf16[2,512,768]{2,1,0:T(8,128)(2,1)} %bitcast.318, bf16[1,4,512,768]{3,2,1,0:T(8,128)(2,1)} %bitcast.302, bf16[1,4,512,768]{3,2,1,0:T(8,128)(2,1)} %bitcast.304, ...), custom_call_target="tpu_custom_call" | custom-call | flops 12000000000 | bytes 1 | tf_op jit(solution)/shard_map/attend_forward/pallas_call | solution.py:175
  98.7 4.0 convolution_convert_fusion.1
  102.7 3.9 convolution_convert_fusion
  106.6 26.2 %attend_forward.3 = (bf16[1,512,768]{2,1,0:T(8,128)(2,1)}, bf16[1,12,512,128]{3,2,1,0:T(8,128)(2,1)}) custom-call(f32[4]{0:T(128)} %add_convert_fusion.9.flags, bf16[2,512,768]{2,1,0:T(8,128)(2,1)} %bitcast.319, bf16[1,4,512,768]{3,2,1,0:T(8,128)(2,1)} %bitcast.283, bf16[1,4,512,768]{3,2,1,0:T(8,128)(2,1)} %bitcast.285, ...), custom_call_target="tpu_custom_call" | custom-call | flops 1 | bytes 1 | tf_op jit(solution)/shard_map/attend_forward/pallas_call | solution.py:175
  135.2 10.2 %collective-permute-done.8.out1 = bf16[768,768]{1,0:T(8,128)(2,1)} collective-permute-done((bf16[768,768]{1,0:T(8,128)(2,1)S(1)}, bf16[768,768]{1,0:T(8,128)(2,1)}, u32[]{:S(2)}, u32[]{:S(2)}) %collective-permute-start.8) | collective-permute-done | bytes 1179680 | tf_op jit(solution)/shard_map/ppermute | solution.py:453
  146.8 3.0 fusion.189
  156.9 4.7 all-to-all-start
  161.6 10.7 %collective-permute-done.11.c = bf16[640,768]{1,0:T(8,128)(2,1)} collective-permute-done((bf16[640,768]{1,0:T(8,128)(2,1)}, bf16[640,768]{1,0:T(8,128)(2,1)}, u32[]{:S(2)}, u32[]{:S(2)}) %collective-permute-start.11) | collective-permute-done | bytes 983072 | tf_op jit(solution)/shard_map/ppermute | solution.py:453
  175.1 24.9 %collective-permute-done.12.in3 = bf16[768,768]{1,0:T(8,128)(2,1)S(1)} collective-permute-done((bf16[768,768]{1,0:T(8,128)(2,1)S(1)}, bf16[768,768]{1,0:T(8,128)(2,1)S(1)}, u32[]{:S(2)}, u32[]{:S(2)}) %collective-permute-start.12) | collective-permute-done | bytes 1179680 | tf_op jit(solution)/shard_map/ppermute | solution.py:453
  203.0 4.4 all-to-all-start.2
  207.5 14.2 %collective-permute-done.10.x = bf16[640,768]{1,0:T(8,128)(2,1)S(1)} collective-permute-done((bf16[640,768]{1,0:T(8,128)(2,1)}, bf16[640,768]{1,0:T(8,128)(2,1)S(1)}, u32[]{:S(2)}, u32[]{:S(2)}) %collective-permute-start.10) | collective-permute-done | bytes 983072 | tf_op jit(solution)/shard_map/ppermute | solution.py:453
  221.7 4.1 collective-permute-done.13.out3
  225.8 19.7 %run_expert.2 = (bf16[4,1280,768]{2,1,0:T(8,128)(2,1)}, bf16[4,1280,768]{2,1,0:T(8,128)(2,1)}, bf16[1280,768]{1,0:T(8,128)(2,1)}, bf16[640,768]{1,0:T(8,128)(2,1...) custom-call(s32[1]{0:T(128)} %bitcast.28.own, bf16[640,768]{1,0:T(8,128)(2,1)} %copy-done.18, ...), custom_call_target="tpu_custom_call" | custom-call | flops 1 | bytes 1 | tf_op jit(solution)/shard_map/run_expert/pallas_call | solution.py:418
  250.0 19.7 %run_expert.3 = (bf16[4,1280,768]{2,1,0:T(8,128)(2,1)}, bf16[4,1280,768]{2,1,0:T(8,128)(2,1)}, bf16[1280,768]{1,0:T(8,128)(2,1)}, bf16[640,768]{1,0:T(8,128)(2,1...) custom-call(s32[1]{0:T(128)} %bitcast.28.own, ...), custom_call_target="tpu_custom_call", output_to_operand_aliasing={{0}: (12, {}), {1}: (13, {}), {2}: (14, {})} | custom-call | flops 1 | bytes 1 | tf_op jit(solution)/shard_map/run_expert/pallas_call | solution.py:418
  272.3 4.6 all-to-all-start.3
  278.5 4.2 fusion.75
  303.8 19.2 %all-to-all-done.3 = bf16[8,160,768]{2,1,0:T(8,128)(2,1)} async-done(((bf16[8,160,768]{2,1,0:T(8,128)(2,1)}), bf16[8,160,768]{2,1,0:T(8,128)(2,1)}, u32[]{:S(2)}, u32[]{:S(2)}) %all-to-all-start.3) | async-done | bytes 1966112 | tf_op jit(solution)/shard_map/all_to_all | solution.py:576
  332.5 4.7 all-to-all-start.4
  337.2 3.9 fusion.66
  342.7 35.4 %attend_backward.2 = (bf16[1,512,768]{2,1,0:T(8,128)(2,1)}, bf16[1,4,512,768]{3,2,1,0:T(8,128)(2,1)}, bf16[1,4,512,768]{3,2,1,0:T(8,128)(2,1)}, f32[1,12,32,128]{3,2,1,0:T(8,128)}) custom-call(f32[4]{0:T(128)} %add_convert_fusion.9.flags, bf16[1,12,512,128]{3,2,1,0:T(8,128)(2,1)} %get-tuple-element.113.qaug, bf16[1,4,512,768]{3,2,1,0:T(8,128)(2,1)} %bitcast.303, ...), custom_call_target="tpu_custom_call" | custom-call | flops 1 | bytes 1 | tf_op jit(solution)/shard_map/attend_backward/pallas_call | solution.py:287
  378.2 35.6 %attend_backward.3 = (bf16[1,512,768]{2,1,0:T(8,128)(2,1)}, bf16[1,4,512,768]{3,2,1,0:T(8,128)(2,1)}, bf16[1,4,512,768]{3,2,1,0:T(8,128)(2,1)}, f32[1,12,32,128]{3,2,1,0:T(8,128)}) custom-call(f32[4]{0:T(128)} %add_convert_fusion.9.flags, bf16[1,12,512,128]{3,2,1,0:T(8,128)(2,1)} %get-tuple-element.134.qaug, bf16[1,4,512,768]{3,2,1,0:T(8,128)(2,1)} %bitcast.284, ...), custom_call_target="tpu_custom_call" | custom-call | flops 1 | bytes 1 | tf_op jit(solution)/shard_map/attend_backward/pallas_call | solution.py:287
  417.0 5.0 convolution_convert_fusion.5
  423.9 4.8 fusion.192
  436.3 3.2 add_convert_fusion.2
  444.2 3.0 add_convert_fusion
  454.4 3.0 convert_add_fusion.1
  461.3 3.3 fusion.14
  465.5 4.5 fusion.196
  470.1 4.9 add_convert_fusion.1
  480.7 4.4 slice_bitcast_fusion
  485.0 8.3 %collective-permute-done.30 = bf16[392,768]{1,0:T(8,128)(2,1)S(1)} collective-permute-done((bf16[392,768]{1,0:T(8,128)(2,1)S(1)}, bf16[392,768]{1,0:T(8,128)(2,1)S(1)}, u32[]{:S(2)}, u32[]{:S(2)}) %collective-permute-start.30) | collective-permute-done | bytes 602144 | tf_op jit(solution)/shard_map/ppermute | solution.py:453
  494.9 11.0 %collective-permute-done.29 = bf16[392,768]{1,0:T(8,128)(2,1)S(1)} collective-permute-done((bf16[392,768]{1,0:T(8,128)(2,1)S(1)}, bf16[392,768]{1,0:T(8,128)(2,1)S(1)}, u32[]{:S(2)}, u32[]{:S(2)}) %collective-permute-start.29) | collective-permute-done | bytes 602144 | tf_op jit(solution)/shard_map/ppermute | solution.py:453
  507.9 3.8 collective-permute-start.33
  516.8 8.4 %collective-permute-done.32 = bf16[98,768]{1,0:T(8,128)(2,1)S(1)} collective-permute-done((bf16[98,768]{1,0:T(8,128)(2,1)S(1)}, bf16[98,768]{1,0:T(8,128)(2,1)S(1)}, u32[]{:S(2)}, u32[]{:S(2)}) %collective-permute-start.32) | collective-permute-done | bytes 150560 | tf_op jit(solution)/shard_map/ppermute | solution.py:457
  529.9 4.4 collective-permute-done.36
  534.6 5.3 collective-permute-done.35
  545.9 27.1 %collective-permute-done.39 = bf16[392,768]{1,0:T(8,128)(2,1)S(1)} collective-permute-done((bf16[392,768]{1,0:T(8,128)(2,1)S(1)}, bf16[392,768]{1,0:T(8,128)(2,1)S(1)}, u32[]{:S(2)}, u32[]{:S(2)}) %collective-permute-start.39) | collective-permute-done | bytes 602144 | tf_op jit(solution)/shard_map/ppermute | solution.py:453
  574.8 4.5 collective-permute-done.38
  579.2 7.0 %collective-permute-done.37 = bf16[392,768]{1,0:T(8,128)(2,1)S(1)} collective-permute-done((bf16[392,768]{1,0:T(8,128)(2,1)S(1)}, bf16[392,768]{1,0:T(8,128)(2,1)S(1)}, u32[]{:S(2)}, u32[]{:S(2)}) %collective-permute-start.37) | collective-permute-done | bytes 602144 | tf_op jit(solution)/shard_map/ppermute | solution.py:453
  589.5 3.6 add_add_fusion
  594.8 7.0 %collective-permute-done.20 = bf16[512,768]{1,0:T(8,128)(2,1)S(1)} collective-permute-done((bf16[512,768]{1,0:T(8,128)(2,1)S(1)}, bf16[512,768]{1,0:T(8,128)(2,1)S(1)}, u32[]{:S(2)}, u32[]{:S(2)}) %collective-permute-start.20) | collective-permute-done | bytes 786464 | tf_op jit(solution)/shard_map/ppermute | solution.py:453
  611.6 7.0 %multiply_reduce_fusion.4 = (f32[768]{0:T(1024)S(1)}, f32[768,768]{1,0:T(8,128)}, f32[768,768]{1,0:T(8,128)}, f32[768]{0:T(1024)S(1)}, f32[768,768]{1,0:T(8,128)}, /*index=5*/f32[768]{0:T(1024)S(1)}, f32[768,768]{1,0:T(8,128)}) fusion(bf16[768,768]{1,0:T(8,128)(2,1)} %param.21, f32[3136,768]{1,0:T(8,128)S(1)} %maximum_convert_fusion, ...), kind=kLoop, calls=%fused_computation.78 | loop fusion | flops 5306112 | bytes 22422528 | tf_op jit(solution)/shard_map/reduce_sum | solution.py:704
  (389 shorter events, 173.4 us)
Async XLA Ops:
  0.6 150.7 %copy-start = (bf16[768,768]{1,0:T(8,128)(2,1)S(1)}, bf16[768,768]{1,0:T(8,128)(2,1)}, u32[]{:S(2)}) copy-start(bf16[768,768]{1,0:T(8,128)(2,1)} %param.23) | copy-start | bytes 3538948
  6.8 45.7 %collective-permute-start = (bf16[512,768]{1,0:T(8,128)(2,1)}, bf16[512,768]{1,0:T(8,128)(2,1)}, u32[]{:S(2)}, u32[]{:S(2)}) collective-permute-start(bf16[512,768]{1,0:T(8,128)(2,1)} %get-tuple-element.303), channel_id=1, source_target_pairs={{0,8},{8,0},{16,24},{24,16},{1,9},{9,1},{17,25},{25,17},{2,10},{10... | collective-permute-start | bytes 2359304 | tf_op jit(solution)/shard_map/ppermute | solution.py:453
  9.7 42.8 %collective-permute-start.1 = (bf16[512,768]{1,0:T(8,128)(2,1)}, bf16[512,768]{1,0:T(8,128)(2,1)}, u32[]{:S(2)}, u32[]{:S(2)}) collective-permute-start(bf16[512,768]{1,0:T(8,128)(2,1)} %get-tuple-element.303), channel_id=1, source_target_pairs={{0,16},{8,24},{16,0},{24,8},{1,17},{9,25},{17,1},{25,9},{2,18},{10... | collective-permute-start | bytes 2359304 | tf_op jit(solution)/shard_map/ppermute | solution.py:453
  11.2 41.3 %collective-permute-start.2 = (bf16[512,768]{1,0:T(8,128)(2,1)}, bf16[512,768]{1,0:T(8,128)(2,1)}, u32[]{:S(2)}, u32[]{:S(2)}) collective-permute-start(bf16[512,768]{1,0:T(8,128)(2,1)} %get-tuple-element.303), channel_id=1, source_target_pairs={{0,24},{8,16},{16,8},{24,0},{1,25},{9,17},{17,9},{25,1},{2,26},{10... | collective-permute-start | bytes 2359304 | tf_op jit(solution)/shard_map/ppermute | solution.py:453
  17.4 129.4 %all-to-all-start.1 = ((bf16[8,160,768]{2,1,0:T(8,128)(2,1)}), bf16[8,160,768]{2,1,0:T(8,128)(2,1)}, u32[]{:S(2)}, u32[]{:S(2)}) async-start(bf16[8,160,768]{2,1,0:T(8,128)(2,1)} %pad_maximum_fusion.9), calls=%async_computation.1 | async-start | bytes 3932160 | tf_op jit(solution)/shard_map/all_to_all | solution.py:576
  54.7 40.8 %collective-permute-start.5 = (bf16[512,768]{1,0:T(8,128)(2,1)S(1)}, bf16[512,768]{1,0:T(8,128)(2,1)}, u32[]{:S(2)}, u32[]{:S(2)}) collective-permute-start(bf16[512,768]{1,0:T(8,128)(2,1)S(1)} %get-tuple-element.102), channel_id=1, source_target_pairs={{0,24},{8,16},{16,8},{24,0},{1,25},{9,17},{17,9},{25,1},{2,26},{10... | collective-permute-start | bytes 2359304 | tf_op jit(solution)/shard_map/ppermute | solution.py:453
  57.2 38.9 %collective-permute-start.4 = (bf16[512,768]{1,0:T(8,128)(2,1)S(1)}, bf16[512,768]{1,0:T(8,128)(2,1)}, u32[]{:S(2)}, u32[]{:S(2)}) collective-permute-start(bf16[512,768]{1,0:T(8,128)(2,1)S(1)} %get-tuple-element.102), channel_id=1, source_target_pairs={{0,16},{8,24},{16,0},{24,8},{1,17},{9,25},{17,1},{25,9},{2,18},{10... | collective-permute-start | bytes 2359304 | tf_op jit(solution)/shard_map/ppermute | solution.py:453
  57.7 38.9 %collective-permute-start.3 = (bf16[512,768]{1,0:T(8,128)(2,1)S(1)}, bf16[512,768]{1,0:T(8,128)(2,1)}, u32[]{:S(2)}, u32[]{:S(2)}) collective-permute-start(bf16[512,768]{1,0:T(8,128)(2,1)S(1)} %get-tuple-element.102), channel_id=1, source_target_pairs={{0,8},{8,0},{16,24},{24,16},{1,9},{9,1},{17,25},{25,17},{2,10},{10... | collective-permute-start | bytes 2359304 | tf_op jit(solution)/shard_map/ppermute | solution.py:453
  92.4 42.8 %collective-permute-start.6 = (bf16[768,768]{1,0:T(8,128)(2,1)S(1)}, bf16[768,768]{1,0:T(8,128)(2,1)S(1)}, u32[]{:S(2)}, u32[]{:S(2)}) collective-permute-start(bf16[768,768]{1,0:T(8,128)(2,1)S(1)} %copy-done.16), channel_id=1, source_target_pairs={{0,8},{8,0},{16,24},{24,16},{1,9},{9,1},{17,25},{25,17},{2,10},{10... | collective-permute-start | bytes 3538952 | tf_op jit(solution)/shard_map/ppermute | solution.py:453
  94.0 41.2 %collective-permute-start.7 = (bf16[768,768]{1,0:T(8,128)(2,1)}, bf16[768,768]{1,0:T(8,128)(2,1)S(1)}, u32[]{:S(2)}, u32[]{:S(2)}) collective-permute-start(bf16[768,768]{1,0:T(8,128)(2,1)} %get-tuple-element.109), channel_id=1, source_target_pairs={{0,16},{8,24},{16,0},{24,8},{1,17},{9,25},{17,1},{25,9},{2,18},{10... | collective-permute-start | bytes 3538952 | tf_op jit(solution)/shard_map/ppermute | solution.py:453
  95.5 49.9 %collective-permute-start.8 = (bf16[768,768]{1,0:T(8,128)(2,1)S(1)}, bf16[768,768]{1,0:T(8,128)(2,1)}, u32[]{:S(2)}, u32[]{:S(2)}) collective-permute-start(bf16[768,768]{1,0:T(8,128)(2,1)S(1)} %copy-done.15), channel_id=1, source_target_pairs={{0,8},{8,0},{16,24},{24,16},{1,9},{9,1},{17,25},{25,17},{2,10},{10... | collective-permute-start | bytes 3538952 | tf_op jit(solution)/shard_map/ppermute | solution.py:453
  96.0 50.8 %collective-permute-start.9 = (bf16[768,768]{1,0:T(8,128)(2,1)}, bf16[768,768]{1,0:T(8,128)(2,1)}, u32[]{:S(2)}, u32[]{:S(2)}) collective-permute-start(bf16[768,768]{1,0:T(8,128)(2,1)} %get-tuple-element.111), channel_id=1, source_target_pairs={{0,16},{8,24},{16,0},{24,8},{1,17},{9,25},{17,1},{25,9},{2,18},{10... | collective-permute-start | bytes 3538952 | tf_op jit(solution)/shard_map/ppermute | solution.py:453
  149.9 22.4 %collective-permute-start.11 = (bf16[640,768]{1,0:T(8,128)(2,1)}, bf16[640,768]{1,0:T(8,128)(2,1)}, u32[]{:S(2)}, u32[]{:S(2)}) collective-permute-start(bf16[640,768]{1,0:T(8,128)(2,1)} %bitcast.33), channel_id=1, source_target_pairs={{0,16},{8,24},{16,0},{24,8},{1,17},{9,25},{17,1},{25,9},{2,18},{10... | collective-permute-start | bytes 2949128 | tf_op jit(solution)/shard_map/ppermute | solution.py:453
  156.9 44.6 %all-to-all-start = ((bf16[8,80,768]{2,1,0:T(8,128)(2,1)}), bf16[8,80,768]{2,1,0:T(8,128)(2,1)}, u32[]{:S(2)}, u32[]{:S(2)}) async-start(bf16[8,80,768]{2,1,0:T(8,128)(2,1)} %bitcast.321), calls=%async_computation | async-start | bytes 1966080 | tf_op jit(solution)/shard_map/all_to_all | solution.py:576
  174.5 25.4 %collective-permute-start.12 = (bf16[768,768]{1,0:T(8,128)(2,1)S(1)}, bf16[768,768]{1,0:T(8,128)(2,1)S(1)}, u32[]{:S(2)}, u32[]{:S(2)}) collective-permute-start(bf16[768,768]{1,0:T(8,128)(2,1)S(1)} %copy-done.23), channel_id=1, source_target_pairs={{0,8},{8,0},{16,24},{24,16},{1,9},{9,1},{17,25},{25,17},{2,10},{10... | collective-permute-start | bytes 3538952 | tf_op jit(solution)/shard_map/ppermute | solution.py:453
  201.0 24.8 %collective-permute-start.13 = (bf16[768,768]{1,0:T(8,128)(2,1)}, bf16[768,768]{1,0:T(8,128)(2,1)}, u32[]{:S(2)}, u32[]{:S(2)}) collective-permute-start(bf16[768,768]{1,0:T(8,128)(2,1)} %collective-permute-done.9.out2), channel_id=1, source_target_pairs={{0,8},{8,0},{16,24},{24,16},{1,9},{9,1},{17,25},{25,17},{2,10},{10... | collective-permute-start | bytes 3538952 | tf_op jit(solution)/shard_map/ppermute | solution.py:453
  201.5 20.2 %collective-permute-start.10 = (bf16[640,768]{1,0:T(8,128)(2,1)}, bf16[640,768]{1,0:T(8,128)(2,1)S(1)}, u32[]{:S(2)}, u32[]{:S(2)}) collective-permute-start(bf16[640,768]{1,0:T(8,128)(2,1)} %bitcast.30), channel_id=1, source_target_pairs={{0,16},{8,24},{16,0},{24,8},{1,17},{9,25},{17,1},{25,9},{2,18},{10... | collective-permute-start | bytes 2949128 | tf_op jit(solution)/shard_map/ppermute | solution.py:453
  203.0 46.0 %all-to-all-start.2 = ((bf16[8,80,768]{2,1,0:T(8,128)(2,1)}), bf16[8,80,768]{2,1,0:T(8,128)(2,1)S(1)}, u32[]{:S(2)}, u32[]{:S(2)}) async-start(bf16[8,80,768]{2,1,0:T(8,128)(2,1)} %bitcast.320), calls=%async_computation.2 | async-start | bytes 1966080 | tf_op jit(solution)/shard_map/all_to_all | solution.py:576
  245.5 24.1 %collective-permute-start.14 = (bf16[640,768]{1,0:T(8,128)(2,1)}, bf16[640,768]{1,0:T(8,128)(2,1)S(1)}, u32[]{:S(2)}, u32[]{:S(2)}) collective-permute-start(bf16[640,768]{1,0:T(8,128)(2,1)} %get-tuple-element.124), channel_id=1, source_target_pairs={{0,16},{8,24},{16,0},{24,8},{1,17},{9,25},{17,1},{25,9},{2,18},{10... | collective-permute-start | bytes 2949128 | tf_op jit(solution)/shard_map/ppermute | solution.py:453
  272.3 50.7 %all-to-all-start.3 = ((bf16[8,160,768]{2,1,0:T(8,128)(2,1)}), bf16[8,160,768]{2,1,0:T(8,128)(2,1)}, u32[]{:S(2)}, u32[]{:S(2)}) async-start(bf16[8,160,768]{2,1,0:T(8,128)(2,1)} %pad_maximum_fusion.10), calls=%async_computation.3 | async-start | bytes 3932160 | tf_op jit(solution)/shard_map/all_to_all | solution.py:576
  276.9 25.5 %collective-permute-start.15 = (bf16[640,768]{1,0:T(8,128)(2,1)}, bf16[640,768]{1,0:T(8,128)(2,1)S(1)}, u32[]{:S(2)}, u32[]{:S(2)}) collective-permute-start(bf16[640,768]{1,0:T(8,128)(2,1)} %get-tuple-element.130), channel_id=1, source_target_pairs={{0,16},{8,24},{16,0},{24,8},{1,17},{9,25},{17,1},{25,9},{2,18},{10... | collective-permute-start | bytes 2949128 | tf_op jit(solution)/shard_map/ppermute | solution.py:453
  286.0 135.9 %collective-permute-start.16 = (bf16[1536,768]{1,0:T(8,128)(2,1)}, bf16[1536,768]{1,0:T(8,128)(2,1)}, u32[]{:S(2)}, u32[]{:S(2)}) collective-permute-start(bf16[1536,768]{1,0:T(8,128)(2,1)} %pad_maximum_fusion.6), channel_id=1, source_target_pairs={{0,8},{8,0},{16,24},{24,16},{1,9},{9,1},{17,25},{25,17},{2,10},{10... | collective-permute-start | bytes 7077896 | tf_op jit(solution)/shard_map/ppermute | solution.py:453
  291.6 130.3 %collective-permute-start.17 = (bf16[1536,768]{1,0:T(8,128)(2,1)}, bf16[1536,768]{1,0:T(8,128)(2,1)}, u32[]{:S(2)}, u32[]{:S(2)}) collective-permute-start(bf16[1536,768]{1,0:T(8,128)(2,1)} %pad_maximum_fusion.7), channel_id=1, source_target_pairs={{0,16},{8,24},{16,0},{24,8},{1,17},{9,25},{17,1},{25,9},{2,18},{10... | collective-permute-start | bytes 7077896 | tf_op jit(solution)/shard_map/ppermute | solution.py:453
  297.7 124.3 %collective-permute-start.18 = (bf16[1536,768]{1,0:T(8,128)(2,1)}, bf16[1536,768]{1,0:T(8,128)(2,1)}, u32[]{:S(2)}, u32[]{:S(2)}) collective-permute-start(bf16[1536,768]{1,0:T(8,128)(2,1)} %pad_maximum_fusion.8), channel_id=1, source_target_pairs={{0,24},{8,16},{16,8},{24,0},{1,25},{9,17},{17,9},{25,1},{2,26},{10... | collective-permute-start | bytes 7077896 | tf_op jit(solution)/shard_map/ppermute | solution.py:453
  332.5 89.5 %all-to-all-start.4 = ((bf16[8,160,768]{2,1,0:T(8,128)(2,1)}), bf16[8,160,768]{2,1,0:T(8,128)(2,1)}, u32[]{:S(2)}, u32[]{:S(2)}) async-start(bf16[8,160,768]{2,1,0:T(8,128)(2,1)} %pad_maximum_fusion.11), calls=%async_computation.4 | async-start | bytes 3932160 | tf_op jit(solution)/shard_map/all_to_all | solution.py:576
  378.2 38.1 %copy-start.84 = (bf16[64]{0:T(256)(128)(2,1)S(1)}, bf16[64]{0:T(256)(128)(2,1)}, u32[]{:S(2)}) copy-start(bf16[64]{0:T(256)(128)(2,1)} %pad.48.clone) | copy-start | bytes 388
  448.3 63.3 %collective-permute-start.23 = (bf16[256,768]{1,0:T(8,128)(2,1)}, bf16[256,768]{1,0:T(8,128)(2,1)}, u32[]{:S(2)}, u32[]{:S(2)}) collective-permute-start(bf16[256,768]{1,0:T(8,128)(2,1)} %get-tuple-element.279), channel_id=1, source_target_pairs={{0,16},{8,24},{16,0},{24,8},{1,17},{9,25},{17,1},{25,9},{2,18},{10... | collective-permute-start | bytes 1179656 | tf_op jit(solution)/shard_map/ppermute | solution.py:453
  448.9 62.8 %collective-permute-start.25 = (bf16[256,768]{1,0:T(8,128)(2,1)}, bf16[256,768]{1,0:T(8,128)(2,1)}, u32[]{:S(2)}, u32[]{:S(2)}) collective-permute-start(bf16[256,768]{1,0:T(8,128)(2,1)} %get-tuple-element.278), channel_id=1, source_target_pairs={{0,8},{8,0},{16,24},{24,16},{1,9},{9,1},{17,25},{25,17},{2,10},{10... | collective-permute-start | bytes 1179656 | tf_op jit(solution)/shard_map/ppermute | solution.py:453
  454.4 20.6 %collective-permute-start.27 = (bf16[1568,768]{1,0:T(8,128)(2,1)}, bf16[1568,768]{1,0:T(8,128)(2,1)S(1)}, u32[]{:S(2)}, u32[]{:S(2)}) collective-permute-start(bf16[1568,768]{1,0:T(8,128)(2,1)} %dynamic-slice_bitcast_fusion), channel_id=1, source_target_pairs={{0,1},{1,0},{2,3},{3,2},{4,5},{5,4},{6,7},{7,6},{8,9},{9,8},{10,11... | collective-permute-start | bytes 7225352 | tf_op jit(solution)/shard_map/ppermute | solution.py:457
  475.9 17.4 %collective-permute-start.30 = (bf16[392,768]{1,0:T(8,128)(2,1)S(1)}, bf16[392,768]{1,0:T(8,128)(2,1)S(1)}, u32[]{:S(2)}, u32[]{:S(2)}) collective-permute-start(bf16[392,768]{1,0:T(8,128)(2,1)S(1)} %get-tuple-element.289), channel_id=1, source_target_pairs={{0,24},{8,16},{16,8},{24,0},{1,25},{9,17},{17,9},{25,1},{2,26},{10... | collective-permute-start | bytes 1806344 | tf_op jit(solution)/shard_map/ppermute | solution.py:453
  478.5 27.4 %collective-permute-start.29 = (bf16[392,768]{1,0:T(8,128)(2,1)S(1)}, bf16[392,768]{1,0:T(8,128)(2,1)S(1)}, u32[]{:S(2)}, u32[]{:S(2)}) collective-permute-start(bf16[392,768]{1,0:T(8,128)(2,1)S(1)} %get-tuple-element.290), channel_id=1, source_target_pairs={{0,16},{8,24},{16,0},{24,8},{1,17},{9,25},{17,1},{25,9},{2,18},{10... | collective-permute-start | bytes 1806344 | tf_op jit(solution)/shard_map/ppermute | solution.py:453
  479.0 28.4 %collective-permute-start.28 = (bf16[392,768]{1,0:T(8,128)(2,1)S(1)}, bf16[392,768]{1,0:T(8,128)(2,1)S(1)}, u32[]{:S(2)}, u32[]{:S(2)}) collective-permute-start(bf16[392,768]{1,0:T(8,128)(2,1)S(1)} %get-tuple-element.288), channel_id=1, source_target_pairs={{0,8},{8,0},{16,24},{24,16},{1,9},{9,1},{17,25},{25,17},{2,10},{10... | collective-permute-start | bytes 1806344 | tf_op jit(solution)/shard_map/ppermute | solution.py:453
  493.3 48.7 %collective-permute-start.19 = (bf16[256,768]{1,0:T(8,128)(2,1)}, bf16[256,768]{1,0:T(8,128)(2,1)}, u32[]{:S(2)}, u32[]{:S(2)}) collective-permute-start(bf16[256,768]{1,0:T(8,128)(2,1)} %get-tuple-element.273), channel_id=1, source_target_pairs={{0,16},{8,24},{16,0},{24,8},{1,17},{9,25},{17,1},{25,9},{2,18},{10... | collective-permute-start | bytes 1179656 | tf_op jit(solution)/shard_map/ppermute | solution.py:453
  505.8 38.0 %collective-permute-start.21 = (bf16[256,768]{1,0:T(8,128)(2,1)}, bf16[256,768]{1,0:T(8,128)(2,1)}, u32[]{:S(2)}, u32[]{:S(2)}) collective-permute-start(bf16[256,768]{1,0:T(8,128)(2,1)} %get-tuple-element.272), channel_id=1, source_target_pairs={{0,8},{8,0},{16,24},{24,16},{1,9},{9,1},{17,25},{25,17},{2,10},{10... | collective-permute-start | bytes 1179656 | tf_op jit(solution)/shard_map/ppermute | solution.py:453
  507.9 8.9 %collective-permute-start.33 = (bf16[98,768]{1,0:T(8,128)(2,1)S(1)}, bf16[98,768]{1,0:T(8,128)(2,1)S(1)}, u32[]{:S(2)}, u32[]{:S(2)}) collective-permute-start(bf16[98,768]{1,0:T(8,128)(2,1)S(1)} %get-tuple-element.309), channel_id=1, source_target_pairs={{0,6},{1,7},{2,4},{3,5},{4,2},{5,3},{6,0},{7,1},{8,14},{9,15},{10,... | collective-permute-start | bytes 451592 | tf_op jit(solution)/shard_map/ppermute | solution.py:457
  511.6 13.6 %collective-permute-start.32 = (bf16[98,768]{1,0:T(8,128)(2,1)S(1)}, bf16[98,768]{1,0:T(8,128)(2,1)S(1)}, u32[]{:S(2)}, u32[]{:S(2)}) collective-permute-start(bf16[98,768]{1,0:T(8,128)(2,1)S(1)} %get-tuple-element.310), channel_id=1, source_target_pairs={{0,4},{1,5},{2,6},{3,7},{4,0},{5,1},{6,2},{7,3},{8,12},{9,13},{10,... | collective-permute-start | bytes 451592 | tf_op jit(solution)/shard_map/ppermute | solution.py:457
  511.7 13.6 %collective-permute-start.31 = (bf16[98,768]{1,0:T(8,128)(2,1)S(1)}, bf16[98,768]{1,0:T(8,128)(2,1)S(1)}, u32[]{:S(2)}, u32[]{:S(2)}) collective-permute-start(bf16[98,768]{1,0:T(8,128)(2,1)S(1)} %get-tuple-element.308), channel_id=1, source_target_pairs={{0,2},{1,3},{2,0},{3,1},{4,6},{5,7},{6,4},{7,5},{8,10},{9,11},{10,... | collective-permute-start | bytes 451592 | tf_op jit(solution)/shard_map/ppermute | solution.py:457
  525.3 9.0 %collective-permute-start.36 = (bf16[98,768]{1,0:T(8,128)(2,1)S(1)}, bf16[98,768]{1,0:T(8,128)(2,1)S(1)}, u32[]{:S(2)}, u32[]{:S(2)}) collective-permute-start(bf16[98,768]{1,0:T(8,128)(2,1)S(1)} %fusion.114), channel_id=1, source_target_pairs={{0,6},{1,7},{2,4},{3,5},{4,2},{5,3},{6,0},{7,1},{8,14},{9,15},{10,... | collective-permute-start | bytes 451592 | tf_op jit(solution)/shard_map/ppermute | solution.py:457
  527.7 12.2 %collective-permute-start.35 = (bf16[98,768]{1,0:T(8,128)(2,1)S(1)}, bf16[98,768]{1,0:T(8,128)(2,1)S(1)}, u32[]{:S(2)}, u32[]{:S(2)}) collective-permute-start(bf16[98,768]{1,0:T(8,128)(2,1)S(1)} %fusion.114), channel_id=1, source_target_pairs={{0,4},{1,5},{2,6},{3,7},{4,0},{5,1},{6,2},{7,3},{8,12},{9,13},{10,... | collective-permute-start | bytes 451592 | tf_op jit(solution)/shard_map/ppermute | solution.py:457
  527.8 12.7 %collective-permute-start.34 = (bf16[98,768]{1,0:T(8,128)(2,1)S(1)}, bf16[98,768]{1,0:T(8,128)(2,1)S(1)}, u32[]{:S(2)}, u32[]{:S(2)}) collective-permute-start(bf16[98,768]{1,0:T(8,128)(2,1)S(1)} %fusion.114), channel_id=1, source_target_pairs={{0,2},{1,3},{2,0},{3,1},{4,6},{5,7},{6,4},{7,5},{8,10},{9,11},{10,... | collective-permute-start | bytes 451592 | tf_op jit(solution)/shard_map/ppermute | solution.py:457
  534.3 58.8 %collective-permute-start.26 = (bf16[512,768]{1,0:T(8,128)(2,1)S(1)}, bf16[512,768]{1,0:T(8,128)(2,1)S(1)}, u32[]{:S(2)}, u32[]{:S(2)}) collective-permute-start(bf16[512,768]{1,0:T(8,128)(2,1)S(1)} %pad_maximum_fusion.16), channel_id=1, source_target_pairs={{0,16},{8,24},{16,0},{24,8},{1,17},{9,25},{17,1},{25,9},{2,18},{10... | collective-permute-start | bytes 2359304 | tf_op jit(solution)/shard_map/ppermute | solution.py:453
  539.9 53.2 %collective-permute-start.24 = (bf16[512,768]{1,0:T(8,128)(2,1)S(1)}, bf16[512,768]{1,0:T(8,128)(2,1)S(1)}, u32[]{:S(2)}, u32[]{:S(2)}) collective-permute-start(bf16[512,768]{1,0:T(8,128)(2,1)S(1)} %pad_maximum_fusion.15), channel_id=1, source_target_pairs={{0,8},{8,0},{16,24},{24,16},{1,9},{9,1},{17,25},{25,17},{2,10},{10... | collective-permute-start | bytes 2359304 | tf_op jit(solution)/shard_map/ppermute | solution.py:453
  540.8 32.3 %collective-permute-start.39 = (bf16[392,768]{1,0:T(8,128)(2,1)S(1)}, bf16[392,768]{1,0:T(8,128)(2,1)S(1)}, u32[]{:S(2)}, u32[]{:S(2)}) collective-permute-start(bf16[392,768]{1,0:T(8,128)(2,1)S(1)} %pad_maximum_fusion.18), channel_id=1, source_target_pairs={{0,24},{8,16},{16,8},{24,0},{1,25},{9,17},{17,9},{25,1},{2,26},{10... | collective-permute-start | bytes 1806344 | tf_op jit(solution)/shard_map/ppermute | solution.py:453
  542.1 37.2 %collective-permute-start.38 = (bf16[392,768]{1,0:T(8,128)(2,1)S(1)}, bf16[392,768]{1,0:T(8,128)(2,1)S(1)}, u32[]{:S(2)}, u32[]{:S(2)}) collective-permute-start(bf16[392,768]{1,0:T(8,128)(2,1)S(1)} %pad_maximum_fusion.18), channel_id=1, source_target_pairs={{0,16},{8,24},{16,0},{24,8},{1,17},{9,25},{17,1},{25,9},{2,18},{10... | collective-permute-start | bytes 1806344 | tf_op jit(solution)/shard_map/ppermute | solution.py:453
  543.8 42.4 %collective-permute-start.37 = (bf16[392,768]{1,0:T(8,128)(2,1)S(1)}, bf16[392,768]{1,0:T(8,128)(2,1)S(1)}, u32[]{:S(2)}, u32[]{:S(2)}) collective-permute-start(bf16[392,768]{1,0:T(8,128)(2,1)S(1)} %pad_maximum_fusion.18), channel_id=1, source_target_pairs={{0,8},{8,0},{16,24},{24,16},{1,9},{9,1},{17,25},{25,17},{2,10},{10... | collective-permute-start | bytes 1806344 | tf_op jit(solution)/shard_map/ppermute | solution.py:453
  573.1 21.7 %collective-permute-start.22 = (bf16[512,768]{1,0:T(8,128)(2,1)S(1)}, bf16[512,768]{1,0:T(8,128)(2,1)S(1)}, u32[]{:S(2)}, u32[]{:S(2)}) collective-permute-start(bf16[512,768]{1,0:T(8,128)(2,1)S(1)} %pad_maximum_fusion.14), channel_id=1, source_target_pairs={{0,16},{8,24},{16,0},{24,8},{1,17},{9,25},{17,1},{25,9},{2,18},{10... | collective-permute-start | bytes 2359304 | tf_op jit(solution)/shard_map/ppermute | solution.py:453
  579.2 22.6 %collective-permute-start.20 = (bf16[512,768]{1,0:T(8,128)(2,1)S(1)}, bf16[512,768]{1,0:T(8,128)(2,1)S(1)}, u32[]{:S(2)}, u32[]{:S(2)}) collective-permute-start(bf16[512,768]{1,0:T(8,128)(2,1)S(1)} %pad_maximum_fusion.13), channel_id=1, source_target_pairs={{0,8},{8,0},{16,24},{24,16},{1,9},{9,1},{17,25},{25,17},{2,10},{10... | collective-permute-start | bytes 2359304 | tf_op jit(solution)/shard_map/ppermute | solution.py:453
  587.2 20.7 %collective-permute-start.40 = (bf16[1568,768]{1,0:T(8,128)(2,1)S(1)}, bf16[1568,768]{1,0:T(8,128)(2,1)S(1)}, u32[]{:S(2)}, u32[]{:S(2)}) collective-permute-start(bf16[1568,768]{1,0:T(8,128)(2,1)S(1)} %get-tuple-element.282), channel_id=1, source_target_pairs={{0,1},{1,0},{2,3},{3,2},{4,5},{5,4},{6,7},{7,6},{8,9},{9,8},{10,11... | collective-permute-start | bytes 7225352 | tf_op jit(solution)/shard_map/ppermute | solution.py:457
  (90 other events, 611.9 us)
